TPU v7x, 256 devices: a whole 4x4x8 slice. The times are simulated.
256 devices in a mesh: gz: 32 (over z_hi, y, core), gy: 8 (over z_lo, x).
Axes of the slice: x: 4, y: 4, z: 8 (z_hi: 4, z_lo: 2; z = z_hi * 2 + z_lo), core: 2. Of those that a mesh axis runs over, the one named last changes fastest.
Arguments:
- raw_planes: bfloat16 [256, 1024, 1024], P('gz', None, 'gy'), may hold values from 0 to 41, as said below
- slot_plane: int32 [256], P('gz'), may hold values from -1 to 127, as said below
- shear_offsets: int32 [128], replicated, may hold values from 0 to 255
- dark_level: float32 [128], replicated, may hold values from 0.2 to 1
- profile_z: float32 [2, 41], replicated, may hold values from 0.005 to 0.05
- profile_x: float32 [2, 15], replicated, may hold values from 0.02 to 0.15
- profile_y: float32 [2, 15], replicated, may hold values from 0.02 to 0.15
Outputs:
- estimate: float32 [128, 1024, 1024], P('gz', None, 'gy')
Inputs may be any that keep to these rules, and one draw needn't show every extreme that they name: `slot_plane`: every plane 0 to 127 stands in exactly one slot and a slot without a plane holds -1. The 8 slots of one index of gz hold at most 8 planes, in no fixed slot order, and some index holds exactly 8 in every draw. The planes of one index are consecutive numbers, and higher indices hold higher planes. `raw_planes`: nonnegative camera counts.
All inputs are finite; a program needn't handle non-finite values.
Results may differ from a plain program's by a relative error of at most 0.00055.
Values may be sent and summed in bfloat16 or wider, within the bound.
A program may use at most 128 MiB of HBM per device.

v0:
```python
import jax
import jax.numpy as jnp
from jax import lax
from jax.sharding import PartitionSpec as P

KX = 15
ITERS = 2
SHEAR = 256


def with_halo(cells, sides, width):
    for axis, dim in sides:
        count = lax.axis_size(axis)
        ends = count - 1
        head = lax.slice_in_dim(cells, 0, width, axis=dim)
        tail = lax.slice_in_dim(cells, cells.shape[dim] - width, cells.shape[dim], axis=dim)
        cells = jnp.concatenate(
            [
                lax.ppermute(tail, axis, [(i, (i + 1) % count) for i in range(ends)]),
                cells,
                lax.ppermute(head, axis, [((i + 1) % count, i) for i in range(ends)]),
            ],
            axis=dim,
        )
    return cells


def banded(weights, out_len, in_len, shift, mirror):
    extent = weights.shape[1]
    kernel = weights[:, ::-1] if mirror else weights
    out_index = jnp.arange(out_len, dtype=jnp.int32)[:, None]
    in_index = jnp.arange(in_len, dtype=jnp.int32)[None, :]
    distance = in_index - out_index + shift
    taps = jnp.arange(extent, dtype=jnp.int32)
    onehot = (distance[:, :, None] == taps[None, None, :]).astype(jnp.float32)
    return jnp.einsum("oit,rt->roi", onehot, kernel, precision=lax.Precision.HIGHEST)


def operator(volume, profile_z, profile_x, profile_y, mirror):
    depth, width, rows = volume.shape
    half_depth = profile_z.shape[1] // 2
    out_width = width - profile_x.shape[1] + 1
    out_rows = rows - profile_y.shape[1] + 1
    matrix_z = banded(profile_z, depth, depth, half_depth, mirror)
    matrix_x = banded(profile_x, out_width, width, 0, mirror)
    matrix_y = banded(profile_y, out_rows, rows, 0, mirror)
    section = jnp.einsum("roi,ixy->roxy", matrix_z, volume, precision=lax.Precision.HIGHEST)
    section = jnp.einsum("rpx,roxy->ropy", matrix_x, section, precision=lax.Precision.HIGHEST)
    section = jnp.einsum("rqy,ropy->ropq", matrix_y, section, precision=lax.Precision.HIGHEST)
    return jnp.sum(section, axis=0)


def shards(raw_planes, slot_plane, shear_offsets, dark_level, profile_z, profile_x, profile_y):
    capacity, columns, row_count = raw_planes.shape
    groups = lax.axis_size("gz")
    planes = shear_offsets.shape[0]
    matches = slot_plane[:, None] == jnp.arange(planes, dtype=jnp.int32)[None, :]
    offsets = jnp.sum(jnp.where(matches, shear_offsets[None, :], 0), axis=1)
    padded = jnp.pad(raw_planes, ((0, 0), (SHEAR, 0), (0, 0)))
    sheared = jax.vmap(
        lambda one_plane, offset: lax.dynamic_slice_in_dim(one_plane, SHEAR - offset, columns, 0)
    )(padded, offsets)
    labels = jnp.broadcast_to(slot_plane[:, None], (capacity, groups))
    received, owners = (
        lax.all_to_all(sheared, "gz", split_axis=1, concat_axis=0, tiled=True),
        lax.all_to_all(labels, "gz", split_axis=1, concat_axis=0, tiled=True),
    )
    local_cols = received.shape[1]
    placement = (jnp.arange(planes, dtype=jnp.int32)[:, None] == owners[:, 0][None, :]).astype(
        jnp.bfloat16
    )
    observed = jnp.dot(
        placement, received.reshape(received.shape[0], -1), preferred_element_type=jnp.float32
    )
    observed = observed.reshape(planes, local_cols, row_count)
    dark_col = dark_level[:, None, None]
    estimate = observed + dark_col
    half_width = KX // 2
    for iteration in range(ITERS):
        widened = with_halo(
            estimate.astype(jnp.bfloat16), (("gz", 1), ("gy", 2)), half_width
        ).astype(estimate.dtype)
        blurred = operator(widened, profile_z, profile_x, profile_y, True) + dark_col
        quotient = observed / blurred
        quotient_wide = with_halo(
            quotient.astype(jnp.bfloat16), (("gz", 1), ("gy", 2)), half_width
        ).astype(quotient.dtype)
        estimate = estimate * operator(quotient_wide, profile_z, profile_x, profile_y, False)
    return lax.all_to_all(estimate, "gz", split_axis=0, concat_axis=1, tiled=True)


def solution(mesh):
    in_specs = (P("gz", None, "gy"), P("gz"), P(), P(), P(), P(), P())
    out_specs = P("gz", None, "gy")
    return jax.shard_map(shards, mesh=mesh, in_specs=in_specs, out_specs=out_specs, check_vma=False)
```

profile of v0, /device:TPU:33, one launch (start us, length us, event | category | flops | bytes accessed | tf_op | source)
XLA Modules:
  0.0 455.1 jit_solution(8837817797657497558)
XLA Ops:
  1.3 11.0 %all-to-all-start = ((s32[8,32,1]{0,2,1:T(1,128)}), s32[8,32,1]{0,2,1:T(1,128)S(1)}, u32[]{:S(2)}, u32[]{:S(2)}) async-start(s32[8,32,1]{0,2,1:T(1,128)} %broadcast_in_dim.14), calls=%async_computation | async-start | bytes 32768 | tf_op jit(solution)/shard_map/all_to_all | solution.py:66
  15.0 21.7 %while.1 = (s32[]{:T(128)}, bf16[8,1280,128]{2,1,0:T(8,128)(2,1)S(1)}, s32[8,3]{0,1:T(4,128)S(1)}, bf16[8,1024,128]{2,1,0:T(8,128)(2,1)}, s32[]{:T(128)}) while((s32[]{:T(128)}, bf16[8,1280,128]{2,1,0:T(8,128)(2,1)S(1)}, s32[8,3]{0,1:T(4,128)S(1)}, bf16[8,1024,128]{2,1,0:T(8,128)(2,1)}, s32[]{:T(128)}) %tuple.29), condition=%wide.while_cond, body=%wide.while_body.sunk | while | flops 2 | bytes 525429 | solution.py:61
  15.7 2.0 dynamic-slice_dynamic-update-slice_fusion.2
  18.4 2.0 dynamic-slice_dynamic-update-slice_fusion.2
  21.1 2.0 dynamic-slice_dynamic-update-slice_fusion.2
  23.8 2.0 dynamic-slice_dynamic-update-slice_fusion.2
  26.5 2.0 dynamic-slice_dynamic-update-slice_fusion.2
  29.2 2.0 dynamic-slice_dynamic-update-slice_fusion.2
  32.0 2.0 dynamic-slice_dynamic-update-slice_fusion.2
  34.7 2.0 dynamic-slice_dynamic-update-slice_fusion.2
  36.7 4.3 copy.74
  41.1 9.8 %all-to-all-start.1 = ((bf16[8,1024,128]{2,0,1:T(8,128)(2,1)}), bf16[8,1024,128]{2,0,1:T(8,128)(2,1)S(1)}, u32[]{:S(2)}, u32[]{:S(2)}) async-start(bf16[8,1024,128]{2,0,1:T(8,128)(2,1)} %copy.74), calls=%async_computation.1 | async-start | bytes 4194304 | tf_op jit(solution)/shard_map/all_to_all | solution.py:65
  53.6 49.2 %all-to-all-done.1 = bf16[8,1024,128]{2,0,1:T(8,128)(2,1)S(1)} async-done(((bf16[8,1024,128]{2,0,1:T(8,128)(2,1)}), bf16[8,1024,128]{2,0,1:T(8,128)(2,1)S(1)}, u32[]{:S(2)}, u32[]{:S(2)}) %all-to-all-start.1) | async-done | bytes 2097184 | tf_op jit(solution)/shard_map/all_to_all | solution.py:65
  104.3 2.5 copy.76
  106.8 2.3 add_convert_fusion
  109.1 2.6 collective-permute-start
  111.7 1.9 collective-permute-start.1
  114.7 4.4 collective-permute-done.1
  119.1 3.1 collective-permute-start.2
  122.3 4.5 collective-permute-start.3
  128.1 5.7 %fusion.14 = f32[2,128,46,142]{1,3,2,0:T(8,128)} fusion(bf16[128,46,7]{0,2,1:T(8,128)(2,1)S(1)} %collective-permute-done.3, bf16[128,7,128]{0,2,1:T(8,128)(2,1)S(1)} %collective-permute-done.1, bf16[128,32,128]{0,2,1:T(8,128)(2,1)S(1)} %get-tuple-element.39, bf16[128,7,128]{0,2,1:T(8,128)(2,1)S(1)} %collective-permute-done, ...), kind=kOutput, calls=%fused_computation.29 | convolution fusion | flops 2576847872 | bytes 8492032 | tf_op jit(solution)/shard_map/roi,ixy->roxy/dot_general | solution.py:47
  133.8 12.5 %copy.78 = f32[2,128,46,142]{3,2,1,0:T(8,128)} copy(f32[2,128,46,142]{1,3,2,0:T(8,128)} %fusion.14) | data formatting | bytes 13377536 | tf_op jit(solution)/shard_map/roi,ixy->roxy/dot_general | solution.py:47
  146.3 14.3 %convolution_bitcast_fusion.3 = f32[2,128,32,142]{3,2,1,0:T(8,128)S(1)} fusion(f32[2,128,46,142]{3,2,1,0:T(8,128)} %copy.78, f32[2,32,46,1]{2,0,1,3:T(2,128)S(1)} %convolution_bitcast_fusion.5), kind=kOutput, calls=%fused_computation.13 | convolution fusion | flops 642121728 | bytes 11353600 | tf_op jit(solution)/shard_map/rpx,roxy->ropy/dot_general | solution.py:48
  160.7 13.6 %fusion.13 = bf16[128,32,128]{0,2,1:T(8,128)(2,1)S(1)} fusion(f32[128,32,128]{0,2,1:T(8,128)S(1)} %get-tuple-element.40, f32[2,128,32,142]{3,2,1,0:T(8,128)S(1)} %convolution_bitcast_fusion.3, f32[128]{0:T(128)S(1)} %copy-done.1, f32[2,128,142]{1,0,2:T(2,128)S(1)} %fusion.62), kind=kOutput, calls=%fused_computation.25 | convolution fusion | flops 1788346368 | bytes 7944704 | tf_op jit(solution)/shard_map/rqy,ropy->ropq/dot_general | solution.py:49
  174.3 3.1 collective-permute-start.4
  180.4 4.4 collective-permute-done.5
  184.8 2.9 collective-permute-start.6
  187.8 5.2 %collective-permute-start.7 = (bf16[128,46,7]{0,2,1:T(8,128)(2,1)S(1)}, bf16[128,46,7]{0,2,1:T(8,128)(2,1)S(1)}, u32[]{:S(2)}, u32[]{:S(2)}) collective-permute-start(bf16[128,46,7]{0,2,1:T(8,128)(2,1)S(1)} %get-tuple-element.28), channel_id=1, source_target_pairs={{1,0},{2,1},{3,2},{4,3},{5,4},{6,5},{7,6},{9,8},{10,9},{11,10},{12... | collective-permute-start | bytes 247304 | tf_op jit(solution)/shard_map/ppermute | solution.py:21
  194.6 5.7 %fusion.23 = f32[2,128,46,142]{1,3,2,0:T(8,128)} fusion(bf16[128,46,7]{0,2,1:T(8,128)(2,1)S(1)} %collective-permute-done.7, bf16[128,7,128]{0,2,1:T(8,128)(2,1)S(1)} %collective-permute-done.5, bf16[128,32,128]{0,2,1:T(8,128)(2,1)S(1)} %fusion.13, bf16[128,7,128]{0,2,1:T(8,128)(2,1)S(1)} %collective-permute-done.4, ...), kind=kOutput, calls=%fused_computation.39 | convolution fusion | flops 2576847872 | bytes 8492032 | tf_op jit(solution)/shard_map/roi,ixy->roxy/dot_general | solution.py:47
  200.2 12.5 %copy.83 = f32[2,128,46,142]{3,2,1,0:T(8,128)} copy(f32[2,128,46,142]{1,3,2,0:T(8,128)} %fusion.23) | data formatting | bytes 13377536 | tf_op jit(solution)/shard_map/roi,ixy->roxy/dot_general | solution.py:47
  212.8 14.1 %convolution_bitcast_fusion.2 = f32[2,128,32,142]{3,2,1,0:T(8,128)S(1)} fusion(f32[2,128,46,142]{3,2,1,0:T(8,128)} %copy.83, f32[2,32,46,1]{2,0,1,3:T(2,128)S(1)} %convolution_bitcast_fusion.4), kind=kOutput, calls=%fused_computation.12 | convolution fusion | flops 642121728 | bytes 11353600 | tf_op jit(solution)/shard_map/rpx,roxy->ropy/dot_general | solution.py:48
  226.9 14.9 %fusion.105 = (bf16[128,32,128]{0,2,1:T(8,128)(2,1)S(1)}, f32[128,32,128]{0,2,1:T(8,128)}) fusion(f32[2,128,142]{1,0,2:T(2,128)S(1)} %fusion.63, f32[2,128,32,142]{3,2,1,0:T(8,128)S(1)} %convolution_bitcast_fusion.2, f32[128,32,128]{0,2,1:T(8,128)S(1)} %get-tuple-element.40, f32[128]{0:T(128)S(1)} %copy-done.1), kind=kOutput, calls=%fused_computation.139 | convolution fusion | flops 1788346368 | bytes 10041856 | tf_op jit(solution)/shard_map/rqy,ropy->ropq/dot_general | solution.py:49
  242.3 2.8 collective-permute-start.8
  248.0 4.4 collective-permute-done.9
  254.4 6.2 %collective-permute-start.11 = (bf16[128,46,7]{0,2,1:T(8,128)(2,1)S(1)}, bf16[128,46,7]{0,2,1:T(8,128)(2,1)S(1)}, u32[]{:S(2)}, u32[]{:S(2)}) collective-permute-start(bf16[128,46,7]{0,2,1:T(8,128)(2,1)S(1)} %get-tuple-element.26), channel_id=1, source_target_pairs={{1,0},{2,1},{3,2},{4,3},{5,4},{6,5},{7,6},{9,8},{10,9},{11,10},{12... | collective-permute-start | bytes 247304 | tf_op jit(solution)/shard_map/ppermute | solution.py:21
  262.2 5.7 %fusion.32 = f32[2,128,46,142]{1,3,2,0:T(8,128)} fusion(bf16[128,46,7]{0,2,1:T(8,128)(2,1)S(1)} %collective-permute-done.11, bf16[128,7,128]{0,2,1:T(8,128)(2,1)S(1)} %collective-permute-done.9, bf16[128,32,128]{0,2,1:T(8,128)(2,1)S(1)} %get-tuple-element.41, bf16[128,7,128]{0,2,1:T(8,128)(2,1)S(1)} %collective-permute-done.8, ...), kind=kOutput, calls=%fused_computation.49 | convolution fusion | flops 2576847872 | bytes 8492032 | tf_op jit(solution)/shard_map/roi,ixy->roxy/dot_general | solution.py:47
  267.9 12.5 %copy.88 = f32[2,128,46,142]{3,2,1,0:T(8,128)} copy(f32[2,128,46,142]{1,3,2,0:T(8,128)} %fusion.32) | data formatting | bytes 13377536 | tf_op jit(solution)/shard_map/roi,ixy->roxy/dot_general | solution.py:47
  280.4 14.1 %convolution_bitcast_fusion.1 = f32[2,128,32,142]{3,2,1,0:T(8,128)S(1)} fusion(f32[2,128,46,142]{3,2,1,0:T(8,128)} %copy.88, f32[2,32,46,1]{2,0,1,3:T(2,128)S(1)} %convolution_bitcast_fusion.5), kind=kOutput, calls=%fused_computation.11 | convolution fusion | flops 642121728 | bytes 11353600 | tf_op jit(solution)/shard_map/rpx,roxy->ropy/dot_general | solution.py:48
  294.5 13.6 %fusion.11 = bf16[128,32,128]{0,2,1:T(8,128)(2,1)S(1)} fusion(f32[128,32,128]{0,2,1:T(8,128)S(1)} %get-tuple-element.40, f32[2,128,32,142]{3,2,1,0:T(8,128)S(1)} %convolution_bitcast_fusion.1, f32[128]{0:T(128)S(1)} %copy-done.1, f32[2,128,142]{1,0,2:T(2,128)S(1)} %fusion.62), kind=kOutput, calls=%fused_computation.21 | convolution fusion | flops 1788346368 | bytes 7944704 | tf_op jit(solution)/shard_map/rqy,ropy->ropq/dot_general | solution.py:49
  308.2 2.8 collective-permute-start.12
  314.0 4.9 %collective-permute-done.13 = bf16[128,7,128]{0,2,1:T(8,128)(2,1)S(1)} collective-permute-done((bf16[128,7,128]{0,2,1:T(8,128)(2,1)S(1)}, bf16[128,7,128]{0,2,1:T(8,128)(2,1)S(1)}, u32[]{:S(2)}, u32[]{:S(2)}) %collective-permute-start.13) | collective-permute-done | bytes 229408 | tf_op jit(solution)/shard_map/ppermute | solution.py:21
  320.9 7.0 %collective-permute-start.15 = (bf16[128,46,7]{0,2,1:T(8,128)(2,1)S(1)}, bf16[128,46,7]{0,2,1:T(8,128)(2,1)S(1)}, u32[]{:S(2)}, u32[]{:S(2)}) collective-permute-start(bf16[128,46,7]{0,2,1:T(8,128)(2,1)S(1)} %get-tuple-element.24), channel_id=1, source_target_pairs={{1,0},{2,1},{3,2},{4,3},{5,4},{6,5},{7,6},{9,8},{10,9},{11,10},{12... | collective-permute-start | bytes 247304 | tf_op jit(solution)/shard_map/ppermute | solution.py:21
  329.4 5.7 %fusion.41 = f32[2,128,46,142]{1,3,2,0:T(8,128)} fusion(bf16[128,46,7]{0,2,1:T(8,128)(2,1)S(1)} %collective-permute-done.15, bf16[128,7,128]{0,2,1:T(8,128)(2,1)S(1)} %collective-permute-done.13, bf16[128,32,128]{0,2,1:T(8,128)(2,1)S(1)} %fusion.11, bf16[128,7,128]{0,2,1:T(8,128)(2,1)S(1)} %collective-permute-done.12, ...), kind=kOutput, calls=%fused_computation.59 | convolution fusion | flops 2576847872 | bytes 8492032 | tf_op jit(solution)/shard_map/roi,ixy->roxy/dot_general | solution.py:47
  335.1 12.5 %copy.93 = f32[2,128,46,142]{3,2,1,0:T(8,128)} copy(f32[2,128,46,142]{1,3,2,0:T(8,128)} %fusion.41) | data formatting | bytes 13377536 | tf_op jit(solution)/shard_map/roi,ixy->roxy/dot_general | solution.py:47
  347.7 14.3 %convolution_bitcast_fusion = f32[2,128,32,142]{3,2,1,0:T(8,128)S(1)} fusion(f32[2,128,46,142]{3,2,1,0:T(8,128)} %copy.93, f32[2,32,46,1]{2,0,1,3:T(2,128)S(1)} %convolution_bitcast_fusion.4), kind=kOutput, calls=%fused_computation.10 | convolution fusion | flops 642121728 | bytes 11353600 | tf_op jit(solution)/shard_map/rpx,roxy->ropy/dot_general | solution.py:48
  362.0 13.6 %bitcast_multiply_fusion = f32[128,32,128]{0,2,1:T(8,128)S(1)} fusion(f32[128,32,128]{0,2,1:T(8,128)S(1)} %copy-done, f32[2,128,32,142]{3,2,1,0:T(8,128)S(1)} %convolution_bitcast_fusion, f32[2,128,142]{1,0,2:T(2,128)S(1)} %fusion.63), kind=kOutput, calls=%fused_computation.18 | convolution fusion | flops 1787297792 | bytes 8992768 | tf_op jit(solution)/shard_map/rqy,ropy->ropq/dot_general | solution.py:49
  375.6 2.0 copy.98
  377.6 75.6 %all_to_all.46 = f32[128,32,128]{2,1,0:T(8,128)S(1)} all-to-all(f32[128,32,128]{2,1,0:T(8,128)} %copy.98), channel_id=1, replica_groups=mesh['gz'=32,'gy'=8] {'gz'}, dimensions={0} | all-to-all | bytes 4194304 | tf_op jit(solution)/shard_map/all_to_all | solution.py:89
  (76 shorter events, 35.5 us)
Async XLA Ops:
  1.3 39.8 %all-to-all-start = ((s32[8,32,1]{0,2,1:T(1,128)}), s32[8,32,1]{0,2,1:T(1,128)S(1)}, u32[]{:S(2)}, u32[]{:S(2)}) async-start(s32[8,32,1]{0,2,1:T(1,128)} %broadcast_in_dim.14), calls=%async_computation | async-start | bytes 32768 | tf_op jit(solution)/shard_map/all_to_all | solution.py:66
  36.7 14.1 %copy-start.2 = (f32[2,41]{1,0:T(2,128)S(1)}, f32[2,41]{1,0:T(2,128)}, u32[]{:S(2)}) copy-start(f32[2,41]{1,0:T(2,128)} %param.11) | copy-start | bytes 988
  36.7 14.2 %copy-start.4 = (f32[2,15]{1,0:T(2,128)S(1)}, f32[2,15]{1,0:T(2,128)}, u32[]{:S(2)}) copy-start(f32[2,15]{1,0:T(2,128)} %param.12) | copy-start | bytes 364
  36.7 14.3 %copy-start.3 = (f32[2,15]{1,0:T(2,128)S(1)}, f32[2,15]{1,0:T(2,128)}, u32[]{:S(2)}) copy-start(f32[2,15]{1,0:T(2,128)} %param.13) | copy-start | bytes 364
  41.1 61.8 %all-to-all-start.1 = ((bf16[8,1024,128]{2,0,1:T(8,128)(2,1)}), bf16[8,1024,128]{2,0,1:T(8,128)(2,1)S(1)}, u32[]{:S(2)}, u32[]{:S(2)}) async-start(bf16[8,1024,128]{2,0,1:T(8,128)(2,1)} %copy.74), calls=%async_computation.1 | async-start | bytes 4194304 | tf_op jit(solution)/shard_map/all_to_all | solution.py:65
  103.3 3.5 copy-start.1
  109.1 5.6 %collective-permute-start = (bf16[128,7,128]{0,2,1:T(8,128)(2,1)S(1)}, bf16[128,7,128]{0,2,1:T(8,128)(2,1)S(1)}, u32[]{:S(2)}, u32[]{:S(2)}) collective-permute-start(bf16[128,7,128]{0,2,1:T(8,128)(2,1)S(1)} %get-tuple-element.37), channel_id=1, source_target_pairs={{0,8},{8,16},{16,24},{24,32},{32,40},{40,48},{48,56},{56,64},{64,7... | collective-permute-start | bytes 688136 | tf_op jit(solution)/shard_map/ppermute | solution.py:19
  111.7 7.3 %collective-permute-start.1 = (bf16[128,7,128]{0,2,1:T(8,128)(2,1)S(1)}, bf16[128,7,128]{0,2,1:T(8,128)(2,1)S(1)}, u32[]{:S(2)}, u32[]{:S(2)}) collective-permute-start(bf16[128,7,128]{0,2,1:T(8,128)(2,1)S(1)} %get-tuple-element.38), channel_id=1, source_target_pairs={{8,0},{16,8},{24,16},{32,24},{40,32},{48,40},{56,48},{64,56},{72,6... | collective-permute-start | bytes 688136 | tf_op jit(solution)/shard_map/ppermute | solution.py:21
  119.1 7.8 %collective-permute-start.2 = (bf16[128,46,7]{0,2,1:T(8,128)(2,1)S(1)}, bf16[128,46,7]{0,2,1:T(8,128)(2,1)S(1)}, u32[]{:S(2)}, u32[]{:S(2)}) collective-permute-start(bf16[128,46,7]{0,2,1:T(8,128)(2,1)S(1)} %get-tuple-element.29), channel_id=1, source_target_pairs={{0,1},{1,2},{2,3},{3,4},{4,5},{5,6},{6,7},{8,9},{9,10},{10,11},{11... | collective-permute-start | bytes 247304 | tf_op jit(solution)/shard_map/ppermute | solution.py:19
  122.3 5.9 %collective-permute-start.3 = (bf16[128,46,7]{0,2,1:T(8,128)(2,1)S(1)}, bf16[128,46,7]{0,2,1:T(8,128)(2,1)S(1)}, u32[]{:S(2)}, u32[]{:S(2)}) collective-permute-start(bf16[128,46,7]{0,2,1:T(8,128)(2,1)S(1)} %get-tuple-element.30), channel_id=1, source_target_pairs={{1,0},{2,1},{3,2},{4,3},{5,4},{6,5},{7,6},{9,8},{10,9},{11,10},{12... | collective-permute-start | bytes 247304 | tf_op jit(solution)/shard_map/ppermute | solution.py:21
  174.3 6.1 %collective-permute-start.4 = (bf16[128,7,128]{0,2,1:T(8,128)(2,1)S(1)}, bf16[128,7,128]{0,2,1:T(8,128)(2,1)S(1)}, u32[]{:S(2)}, u32[]{:S(2)}) collective-permute-start(bf16[128,7,128]{0,2,1:T(8,128)(2,1)S(1)} %get-tuple-element.35), channel_id=1, source_target_pairs={{0,8},{8,16},{16,24},{24,32},{32,40},{40,48},{48,56},{56,64},{64,7... | collective-permute-start | bytes 688136 | tf_op jit(solution)/shard_map/ppermute | solution.py:19
  177.4 7.3 %collective-permute-start.5 = (bf16[128,7,128]{0,2,1:T(8,128)(2,1)S(1)}, bf16[128,7,128]{0,2,1:T(8,128)(2,1)S(1)}, u32[]{:S(2)}, u32[]{:S(2)}) collective-permute-start(bf16[128,7,128]{0,2,1:T(8,128)(2,1)S(1)} %get-tuple-element.36), channel_id=1, source_target_pairs={{8,0},{16,8},{24,16},{32,24},{40,32},{48,40},{56,48},{64,56},{72,6... | collective-permute-start | bytes 688136 | tf_op jit(solution)/shard_map/ppermute | solution.py:21
  184.8 8.4 %collective-permute-start.6 = (bf16[128,46,7]{0,2,1:T(8,128)(2,1)S(1)}, bf16[128,46,7]{0,2,1:T(8,128)(2,1)S(1)}, u32[]{:S(2)}, u32[]{:S(2)}) collective-permute-start(bf16[128,46,7]{0,2,1:T(8,128)(2,1)S(1)} %get-tuple-element.27), channel_id=1, source_target_pairs={{0,1},{1,2},{2,3},{3,4},{4,5},{5,6},{6,7},{8,9},{9,10},{10,11},{11... | collective-permute-start | bytes 247304 | tf_op jit(solution)/shard_map/ppermute | solution.py:19
  187.8 6.8 %collective-permute-start.7 = (bf16[128,46,7]{0,2,1:T(8,128)(2,1)S(1)}, bf16[128,46,7]{0,2,1:T(8,128)(2,1)S(1)}, u32[]{:S(2)}, u32[]{:S(2)}) collective-permute-start(bf16[128,46,7]{0,2,1:T(8,128)(2,1)S(1)} %get-tuple-element.28), channel_id=1, source_target_pairs={{1,0},{2,1},{3,2},{4,3},{5,4},{6,5},{7,6},{9,8},{10,9},{11,10},{12... | collective-permute-start | bytes 247304 | tf_op jit(solution)/shard_map/ppermute | solution.py:21
  242.3 5.8 %collective-permute-start.8 = (bf16[128,7,128]{0,2,1:T(8,128)(2,1)S(1)}, bf16[128,7,128]{0,2,1:T(8,128)(2,1)S(1)}, u32[]{:S(2)}, u32[]{:S(2)}) collective-permute-start(bf16[128,7,128]{0,2,1:T(8,128)(2,1)S(1)} %get-tuple-element.33), channel_id=1, source_target_pairs={{0,8},{8,16},{16,24},{24,32},{32,40},{40,48},{48,56},{56,64},{64,7... | collective-permute-start | bytes 688136 | tf_op jit(solution)/shard_map/ppermute | solution.py:19
  245.1 7.3 %collective-permute-start.9 = (bf16[128,7,128]{0,2,1:T(8,128)(2,1)S(1)}, bf16[128,7,128]{0,2,1:T(8,128)(2,1)S(1)}, u32[]{:S(2)}, u32[]{:S(2)}) collective-permute-start(bf16[128,7,128]{0,2,1:T(8,128)(2,1)S(1)} %get-tuple-element.34), channel_id=1, source_target_pairs={{8,0},{16,8},{24,16},{32,24},{40,32},{48,40},{56,48},{64,56},{72,6... | collective-permute-start | bytes 688136 | tf_op jit(solution)/shard_map/ppermute | solution.py:21
  252.5 8.2 %collective-permute-start.10 = (bf16[128,46,7]{0,2,1:T(8,128)(2,1)S(1)}, bf16[128,46,7]{0,2,1:T(8,128)(2,1)S(1)}, u32[]{:S(2)}, u32[]{:S(2)}) collective-permute-start(bf16[128,46,7]{0,2,1:T(8,128)(2,1)S(1)} %get-tuple-element.25), channel_id=1, source_target_pairs={{0,1},{1,2},{2,3},{3,4},{4,5},{5,6},{6,7},{8,9},{9,10},{10,11},{11... | collective-permute-start | bytes 247304 | tf_op jit(solution)/shard_map/ppermute | solution.py:19
  254.4 7.8 %collective-permute-start.11 = (bf16[128,46,7]{0,2,1:T(8,128)(2,1)S(1)}, bf16[128,46,7]{0,2,1:T(8,128)(2,1)S(1)}, u32[]{:S(2)}, u32[]{:S(2)}) collective-permute-start(bf16[128,46,7]{0,2,1:T(8,128)(2,1)S(1)} %get-tuple-element.26), channel_id=1, source_target_pairs={{1,0},{2,1},{3,2},{4,3},{5,4},{6,5},{7,6},{9,8},{10,9},{11,10},{12... | collective-permute-start | bytes 247304 | tf_op jit(solution)/shard_map/ppermute | solution.py:21
  308.2 5.8 %collective-permute-start.12 = (bf16[128,7,128]{0,2,1:T(8,128)(2,1)S(1)}, bf16[128,7,128]{0,2,1:T(8,128)(2,1)S(1)}, u32[]{:S(2)}, u32[]{:S(2)}) collective-permute-start(bf16[128,7,128]{0,2,1:T(8,128)(2,1)S(1)} %get-tuple-element.31), channel_id=1, source_target_pairs={{0,8},{8,16},{16,24},{24,32},{32,40},{40,48},{48,56},{56,64},{64,7... | collective-permute-start | bytes 688136 | tf_op jit(solution)/shard_map/ppermute | solution.py:19
  311.0 7.9 %collective-permute-start.13 = (bf16[128,7,128]{0,2,1:T(8,128)(2,1)S(1)}, bf16[128,7,128]{0,2,1:T(8,128)(2,1)S(1)}, u32[]{:S(2)}, u32[]{:S(2)}) collective-permute-start(bf16[128,7,128]{0,2,1:T(8,128)(2,1)S(1)} %get-tuple-element.32), channel_id=1, source_target_pairs={{8,0},{16,8},{24,16},{32,24},{40,32},{48,40},{56,48},{64,56},{72,6... | collective-permute-start | bytes 688136 | tf_op jit(solution)/shard_map/ppermute | solution.py:21
  318.9 8.9 %collective-permute-start.14 = (bf16[128,46,7]{0,2,1:T(8,128)(2,1)S(1)}, bf16[128,46,7]{0,2,1:T(8,128)(2,1)S(1)}, u32[]{:S(2)}, u32[]{:S(2)}) collective-permute-start(bf16[128,46,7]{0,2,1:T(8,128)(2,1)S(1)} %get-tuple-element.23), channel_id=1, source_target_pairs={{0,1},{1,2},{2,3},{3,4},{4,5},{5,6},{6,7},{8,9},{9,10},{10,11},{11... | collective-permute-start | bytes 247304 | tf_op jit(solution)/shard_map/ppermute | solution.py:19
  320.9 8.6 %collective-permute-start.15 = (bf16[128,46,7]{0,2,1:T(8,128)(2,1)S(1)}, bf16[128,46,7]{0,2,1:T(8,128)(2,1)S(1)}, u32[]{:S(2)}, u32[]{:S(2)}) collective-permute-start(bf16[128,46,7]{0,2,1:T(8,128)(2,1)S(1)} %get-tuple-element.24), channel_id=1, source_target_pairs={{1,0},{2,1},{3,2},{4,3},{5,4},{6,5},{7,6},{9,8},{10,9},{11,10},{12... | collective-permute-start | bytes 247304 | tf_op jit(solution)/shard_map/ppermute | solution.py:21
  347.7 14.3 %copy-start = (f32[128,32,128]{0,2,1:T(8,128)S(1)}, f32[128,32,128]{0,2,1:T(8,128)}, u32[]{:S(2)}) copy-start(f32[128,32,128]{0,2,1:T(8,128)} %get-tuple-element.42) | copy-start | bytes 6291460
where the time goes:
time: 463 us; the launch traced here: 455 us
  matrix products  142 us (31%)
  local copies, waits for them, and re-layouts  87.6 us (19%)
  waiting for transfers between devices  75.8 us (16%)
  blocking collectives  75.6 us (16%)
  starting transfers between devices  72.6 us (16%)
    all_to_all x1, blocking collectives, shards(): lax.all_to_all(estimate, 'gz', split_axis=0, concat_axis=1, tiled=True)  75.6 us
    dot_general x4, matrix products, operator(): jnp.einsum('rpx,roxy->ropy', matrix_x, section, precision=lax.Precision.H...  56.8 us
    dot_general x4, matrix products, operator(): jnp.einsum('rqy,ropy->ropq', matrix_y, section, precision=lax.Precision.H...  55.8 us
    dot_general x4, local copies, waits for them, and re-layouts, operator(): jnp.einsum('roi,ixy->roxy', matrix_z, volume, precision=lax.Precision.HIG...  50.1 us
    all_to_all x1, waiting for transfers between devices, shards(): lax.all_to_all(sheared, 'gz', split_axis=1, concat_axis=0, tiled=True)  49.2 us
    ppermute x8, starting transfers between devices, with_halo(): lax.ppermute(head, axis, [((i + 1) % count, i) for i in range(ends)])  30.6 us
    ppermute x8, waiting for transfers between devices, with_halo(): lax.ppermute(head, axis, [((i + 1) % count, i) for i in range(ends)])  23.7 us
    dot_general x4, matrix products, operator(): jnp.einsum('roi,ixy->roxy', matrix_z, volume, precision=lax.Precision.HIG...  22.7 us
  transfers between devices with their start and end apart: 18, of which 13 were waited for; matrix products, arithmetic and copies ran while one was open for 7% of the time, Pallas kernels for 0%

commit v1 on v0

v1 whole, which is shorter than its diff:
```python
import jax
import jax.numpy as jnp
from jax import lax
from jax.experimental import pallas as pl
from jax.experimental.pallas import tpu as pltpu
from jax.sharding import PartitionSpec as P

SHEAR = 256
ITERS = 2
NZ = 128
NB = 32
XB = 32
YB = 128
CAP = 8
TX = 15
TZ = 41
MESH = pl.DeviceIdType.MESH
BF = jnp.bfloat16
F32 = jnp.float32
I32 = jnp.int32
V = pl.BlockSpec(memory_space=pltpu.VMEM)
SM = pl.BlockSpec(memory_space=pltpu.SMEM)
ANY = pl.BlockSpec(memory_space=pl.ANY)


def params(mib, **kw):
    return pltpu.CompilerParams(vmem_limit_bytes=mib * 2**20, **kw)


def snake(g):
    high = lax.div(g, 8)
    y = lax.rem(lax.div(g, 2), 4)
    flip = lax.rem(high, 2)
    return high * 8 + (y + flip * (3 - 2 * y)) * 2 + lax.rem(g, 2)


def iota(shape, dim):
    return lax.broadcasted_iota(I32, shape, dim)


def dot(a, b):
    return jnp.dot(a, b, preferred_element_type=F32)


def split(v):
    hi = v.astype(BF)
    return hi, (v - hi.astype(F32)).astype(BF)


def toeplitz(profile, r, distance, extent, mirror):
    total = jnp.zeros(distance.shape, F32)
    for d in range(extent):
        total = jnp.where(distance == d, profile[r, extent - 1 - d if mirror else d], total)
    return total


def tables_kernel(pz, px, py, dark, wy_hi, wy_lo, bz_hl, edges, dark_col):
    for kind in range(2):
        mirror = kind == 0
        for r in range(2):
            lanes = pl.ds(r * 128, 128)
            row = iota((128, 128), 0)
            col = iota((128, 128), 1)
            hi, lo = split(toeplitz(py, r, row - col + 7, TX, mirror))
            for s in range(8):
                wy_hi[kind, s, 0:128, lanes] = hi
                wy_lo[kind, s, 0:128, lanes] = lo
            h = lax.rem(row, 16)
            source = jnp.where(h < 8, h - 7, h + 120)
            distance = jnp.where(lax.rem(h, 8) == 7, -1, source - col + 7)
            halo = toeplitz(py, r, distance, TX, mirror)
            for s in range(8):
                hi, lo = split(jnp.where(lax.div(row, 16) == s, halo, 0.0))
                wy_hi[kind, s, 128:256, lanes] = hi
                wy_lo[kind, s, 128:256, lanes] = lo
            hi, lo = split(toeplitz(pz, r, col - row + TZ // 2, TZ, mirror))
            bz_hl[kind, 0:128, lanes] = hi
            bz_hl[kind, 128:256, lanes] = lo
    row = iota((128, 128), 0)
    col = iota((128, 128), 1)
    for s in range(8):
        near = (col == s * 16 + 8 + row) & (row < 7)
        far = (col == s * 16 + row - 121) & (row >= 121)
        edges[s, :, 0:128] = jnp.where(near, 1.0, 0.0).astype(BF)
        edges[s, :, 128:256] = jnp.where(far, 1.0, 0.0).astype(BF)
    level = jnp.sum(jnp.where(row == col, dark[...], 0.0), axis=1, keepdims=True)
    dark_col[...] = jnp.broadcast_to(level, (128, 128))


def make_tables(profile_z, profile_x, profile_y, dark_level):
    return pl.pallas_call(
        tables_kernel,
        out_shape=[
            jax.ShapeDtypeStruct((2, 8, 256, 256), BF),
            jax.ShapeDtypeStruct((2, 8, 256, 256), BF),
            jax.ShapeDtypeStruct((2, 256, 256), BF),
            jax.ShapeDtypeStruct((8, 128, 256), BF),
            jax.ShapeDtypeStruct((128, 128), F32),
        ],
        in_specs=[SM, SM, SM, V],
        out_specs=[V] * 5,
        compiler_params=params(24),
        name="tables",
    )(profile_z, profile_x, profile_y, dark_level.reshape(1, 128))


def shear_kernel(slot, offsets, raw, blocks, label_row, padded, woven):
    columns = raw.shape[1]
    lane = lax.rem(iota((1, 128), 1), CAP)
    labels = jnp.zeros((1, 128), I32)
    for k in range(2):
        padded[k, 0:SHEAR] = jnp.zeros((SHEAR, 128), F32)
    for c in range(CAP):
        plane = slot[c]
        labels = jnp.where(lane == c, plane, labels)
        start = SHEAR - offsets[jnp.maximum(plane, 0)]
        k = c % 2
        for x in range(0, columns, 256):
            padded[k, SHEAR + x : SHEAR + x + 256] = raw[c, x : x + 256].astype(F32)
        for x in range(0, columns, 256):
            woven[pl.ds(x * CAP + c, 256, stride=CAP), :] = padded[k, pl.ds(start + x, 256), :]
    label_row[...] = labels

    def pack(i, carry):
        at = pl.ds(pl.multiple_of(i * 512, 512), 512)
        blocks[pl.ds(i * 32, 32)] = woven[at, :].reshape(32, 16, 128).astype(BF)
        return carry

    lax.fori_loop(0, columns * CAP // 512, pack, 0)


def shear(slot_plane, shear_offsets, raw):
    columns = raw.shape[1]
    return pl.pallas_call(
        shear_kernel,
        out_shape=[
            jax.ShapeDtypeStruct((columns // 2, 16, 128), BF),
            jax.ShapeDtypeStruct((1, 128), I32),
        ],
        in_specs=[SM, SM, V],
        out_specs=[V, V],
        scratch_shapes=[
            pltpu.VMEM((2, SHEAR + columns, 128), F32),
            pltpu.VMEM((columns * CAP, 128), F32),
        ],
        compiler_params=params(24),
        name="shear",
    )(slot_plane, shear_offsets, raw)


def greet_all(g, q):
    barrier = pltpu.get_barrier_semaphore()

    def hello(k, carry):
        pl.semaphore_signal(barrier, inc=1, device_id=(lax.rem(g + k, NB), q), device_id_type=MESH)
        return carry

    lax.fori_loop(1, NB, hello, 0)
    pl.semaphore_wait(barrier, NB - 1)


def scatter_kernel(blocks, label_row, received, labels, send, recv, send_small, recv_small, own):
    g = lax.axis_index("gz")
    q = lax.axis_index("gy")
    greet_all(g, q)

    def pair(k, target):
        block = snake(target)
        big = pltpu.make_async_remote_copy(
            src_ref=blocks.at[pl.ds(block * 16, 16)],
            dst_ref=received.at[g],
            send_sem=send.at[k],
            recv_sem=recv.at[k],
            device_id=(target, q),
            device_id_type=MESH,
        )
        small = pltpu.make_async_remote_copy(
            src_ref=label_row,
            dst_ref=labels.at[g],
            send_sem=send_small.at[k],
            recv_sem=recv_small.at[k],
            device_id=(target, q),
            device_id_type=MESH,
        )
        return big, small

    def start(k, carry):
        for copy in pair(k, lax.rem(g + k, NB)):
            copy.start()
        return carry

    lax.fori_loop(1, NB, start, 0)
    mine = (
        pltpu.make_async_copy(blocks.at[pl.ds(snake(g) * 16, 16)], received.at[g], own.at[0]),
        pltpu.make_async_copy(label_row, labels.at[g], own.at[1]),
    )
    for copy in mine:
        copy.start()
    for copy in mine:
        copy.wait()

    def finish(k, carry):
        for copy in pair(k, lax.rem(g + k, NB)):
            copy.wait()
        return carry

    lax.fori_loop(1, NB, finish, 0)


def scatter(blocks, label_row):
    return pl.pallas_call(
        scatter_kernel,
        out_shape=[
            jax.ShapeDtypeStruct((NB, 16, 16, 128), BF),
            jax.ShapeDtypeStruct((NB, 1, 128), I32),
        ],
        in_specs=[ANY, ANY],
        out_specs=[ANY, ANY],
        scratch_shapes=[pltpu.SemaphoreType.DMA((NB,))] * 4 + [pltpu.SemaphoreType.DMA((2,))],
        compiler_params=params(8, collective_id=0, has_side_effects=True),
        name="scatter",
    )(blocks, label_row)


def collect_kernel(coded, peak, out, peaks, send, recv, send_small, recv_small, own):
    g = lax.axis_index("gz")
    q = lax.axis_index("gy")
    block = snake(g)
    greet_all(g, q)
    rows = pl.ds(pl.multiple_of(block * XB, XB), XB)

    def pair(k, target):
        big = pltpu.make_async_remote_copy(
            src_ref=coded.at[pl.ds(target * 4, 4)],
            dst_ref=out.at[:, rows, :],
            send_sem=send.at[k],
            recv_sem=recv.at[k],
            device_id=(target, q),
            device_id_type=MESH,
        )
        small = pltpu.make_async_remote_copy(
            src_ref=peak,
            dst_ref=peaks.at[block],
            send_sem=send_small.at[k],
            recv_sem=recv_small.at[k],
            device_id=(target, q),
            device_id_type=MESH,
        )
        return big, small

    def start(k, carry):
        for copy in pair(k, lax.rem(g + k, NB)):
            copy.start()
        return carry

    lax.fori_loop(1, NB, start, 0)
    mine = (
        pltpu.make_async_copy(coded.at[pl.ds(g * 4, 4)], out.at[:, rows, :], own.at[0]),
        pltpu.make_async_copy(peak, peaks.at[block], own.at[1]),
    )
    for copy in mine:
        copy.start()
    for copy in mine:
        copy.wait()

    def finish(k, carry):
        for copy in pair(k, lax.rem(g + k, NB)):
            copy.wait()
        return carry

    lax.fori_loop(1, NB, finish, 0)


def collect(coded, peak):
    return pl.pallas_call(
        collect_kernel,
        out_shape=[
            jax.ShapeDtypeStruct((4, NB * XB, 128), BF),
            jax.ShapeDtypeStruct((NB, 1, 128), F32),
        ],
        in_specs=[ANY, ANY],
        out_specs=[ANY, ANY],
        scratch_shapes=[pltpu.SemaphoreType.DMA((NB,))] * 4 + [pltpu.SemaphoreType.DMA((2,))],
        compiler_params=params(8, collective_id=1, has_side_effects=True),
        name="collect",
    )(coded, peak)


def halo_kernel(faces, packs, x_halo, y_halo, send, recv):
    g = lax.axis_index("gz")
    q = lax.axis_index("gy")
    b = snake(g)
    count = lax.axis_size("gy")
    up, down = snake(lax.rem(b + 1, NB)), snake(lax.rem(b + NB - 1, NB))
    right, left = lax.rem(q + 1, count), lax.rem(q + count - 1, count)
    barrier = pltpu.get_barrier_semaphore()
    around = [(d, e) for d in (down, g, up) for e in (left, q, right)]
    del around[4]
    for device in around:
        pl.semaphore_signal(barrier, inc=1, device_id=device, device_id_type=MESH)
    pl.semaphore_wait(barrier, 8)
    moves = [
        (faces.at[1, pl.ds(1, 7)], x_halo.at[0, pl.ds(1, 7)], (up, q)),
        (faces.at[0, pl.ds(0, 7)], x_halo.at[1, pl.ds(0, 7)], (down, q)),
        (packs.at[1], y_halo.at[0, pl.ds(1, 4)], (g, right)),
        (packs.at[0], y_halo.at[1, pl.ds(1, 4)], (g, left)),
        (packs.at[1, 3], y_halo.at[0, 0], (up, right)),
        (packs.at[1, 0], y_halo.at[0, 5], (down, right)),
        (packs.at[0, 3], y_halo.at[1, 0], (up, left)),
        (packs.at[0, 0], y_halo.at[1, 5], (down, left)),
    ]
    copies = [
        pltpu.make_async_remote_copy(
            src_ref=src, dst_ref=dst, send_sem=send.at[i], recv_sem=recv.at[i], device_id=device, device_id_type=MESH
        )
        for i, (src, dst, device) in enumerate(moves)
    ]
    for copy in copies:
        copy.start()
    for copy in copies:
        copy.wait()


def exchange(faces, packs, collective_id):
    return pl.pallas_call(
        halo_kernel,
        out_shape=[
            jax.ShapeDtypeStruct((2, 8, 128, 128), BF),
            jax.ShapeDtypeStruct((2, 6, 128, 128), BF),
        ],
        in_specs=[ANY, ANY],
        out_specs=[ANY, ANY],
        scratch_shapes=[pltpu.SemaphoreType.DMA((8,))] * 2,
        compiler_params=params(8, collective_id=collective_id, has_side_effects=True),
        name="halo",
    )(faces, packs)


def store_edges(group, values, edges, faces, packs):
    total = dot(values[0], edges[0])
    for s in range(1, 8):
        total += dot(values[s], edges[s])
    packs[0, group] = total[:, 0:128].astype(BF)
    packs[1, group] = total[:, 128:256].astype(BF)

    @pl.when(group == 0)
    def _():
        for s in range(8):
            faces[0, s] = values[s]

    @pl.when(group == 3)
    def _():
        for s in range(8):
            faces[1, s] = values[s]


def place_kernel(received, labels, edges, observed, faces, packs):
    lane = iota((128, 128), 1)
    plane = iota((128, 128), 0)
    parts = []
    for chunk in range(4):
        row = jnp.zeros((1, 128), I32)
        for j in range(8):
            row = jnp.where(lax.div(iota((1, 128), 1), 16) == j, labels[chunk * 8 + j], row)
        parts.append(row == plane)
    parity = lax.rem(lax.div(lane, CAP), 2)
    onehot = jnp.concatenate(
        [
            jnp.concatenate([jnp.where(hit & (parity == p), 1.0, 0.0).astype(BF) for hit in parts], axis=1)
            for p in range(2)
        ],
        axis=0,
    )

    def group(k, carry):
        values = []
        for j in range(4):
            both = dot(onehot, received[:, k * 4 + j].reshape(NB * 16, 128)).astype(BF)
            values += [both[0:128], both[128:256]]
        for s in range(8):
            observed[k * 8 + s] = values[s]
        store_edges(k, values, edges, faces, packs)
        return carry

    lax.fori_loop(0, 4, group, 0)


def place(received, labels, edges):
    return pl.pallas_call(
        place_kernel,
        out_shape=[
            jax.ShapeDtypeStruct((XB, 128, 128), BF),
            jax.ShapeDtypeStruct((2, 8, 128, 128), BF),
            jax.ShapeDtypeStruct((2, 4, 128, 128), BF),
        ],
        in_specs=[V] * 3,
        out_specs=[V] * 3,
        compiler_params=params(24),
        name="place",
    )(received, labels, edges)


def blur_block(main, x_halo, y_halo, px, wy_hi, wy_lo, bz_hl, mirror, dark_col, by_y, x_hi, x_lo, finish):
    b = snake(lax.axis_index("gz"))
    q = lax.axis_index("gy")
    inside = (b > 0, b < NB - 1)
    lane = lax.rem(iota((128, 128), 1), 16)
    outside_y = ((lane < 8) & (q == 0)) | ((lane >= 8) & (q == lax.axis_size("gy") - 1))

    def rows_halo(group):
        both = y_halo[0, group].astype(F32) + y_halo[1, group].astype(F32)
        if dark_col is not None:
            both += dark_col[...]
        return jnp.where(outside_y, 0.0, both)

    def along_y(at, s, v, halo):
        hi, lo = split(v)
        h_hi, h_lo = halo
        wide = jnp.concatenate([hi, h_hi], axis=1)
        total = dot(wide, wy_hi[0, s]) + dot(wide, wy_lo[0, s])
        if h_lo is None:
            total += dot(lo, wy_hi[0, s, 0:128])
        else:
            total += dot(jnp.concatenate([lo, h_lo], axis=1), wy_hi[0, s])
        by_y[at, 0:128] = total[:, 0:128]
        by_y[at, 128:256] = total[:, 128:256]

    def spread(halo):
        if dark_col is not None:
            return split(halo)
        return halo.astype(BF), None

    for side, group, members in ((0, 0, range(1, 8)), (1, 5, range(0, 7))):
        halo = spread(jnp.where(inside[side], rows_halo(group), 0.0))
        for s in members:
            v = x_halo[side, s].astype(F32)
            if dark_col is not None:
                v += dark_col[...]
            along_y(group * 8 + s, s, jnp.where(inside[side], v, 0.0), halo)

    def main_group(k, carry):
        halo = spread(rows_halo(k + 1))
        for s in range(8):
            along_y((k + 1) * 8 + s, s, main(k * 8 + s), halo)
        return carry

    lax.fori_loop(0, 4, main_group, 0)

    def along_x(t, carry):
        for r in range(2):
            rows = pl.ds(pl.multiple_of(r * 128 + t * 16, 16), 16)
            taps = [px[r, TX - 1 - j if mirror else j] for j in range(TX)]
            lines = [by_y[i, rows, :] for i in range(1, 47)]
            for x in range(XB):
                total = taps[0] * lines[x]
                for j in range(1, TX):
                    total += taps[j] * lines[x + j]
                hi, lo = split(total)
                x_hi[x, rows, :] = hi
                x_lo[x, rows, :] = lo
        return carry

    lax.fori_loop(0, 8, along_x, 0)

    def along_z(k, carry):
        results = []
        for j in range(0, 8, 2):
            x = k * 8 + j
            hi = jnp.concatenate([x_hi[x], x_hi[x + 1]], axis=1)
            lo = jnp.concatenate([x_lo[x], x_lo[x + 1]], axis=1)
            both = dot(bz_hl[0], hi)
            total = both[0:128] + both[128:256] + dot(bz_hl[0, 0:128], lo)
            results += [total[:, 0:128], total[:, 128:256]]
        finish(k, results)
        return carry

    lax.fori_loop(0, 4, along_z, 0)


SCRATCH = [
    pltpu.VMEM((48, 256, 128), F32),
    pltpu.VMEM((XB, 256, 128), BF),
    pltpu.VMEM((XB, 256, 128), BF),
]


def ratio_kernel(first, px, estimate, observed, x_halo, y_halo, dark_col, wy_hi, wy_lo, bz_hl, edges, quotient, faces, packs, *scratch):
    def main(x):
        if first:
            return estimate[x].astype(F32) + dark_col[...]
        return estimate[x]

    def finish(k, results):
        values = []
        for s in range(8):
            value = observed[k * 8 + s].astype(F32) / (results[s] + dark_col[...])
            quotient[k * 8 + s] = value
            values.append(value.astype(BF))
        store_edges(k, values, edges, faces, packs)

    blur_block(main, x_halo, y_halo, px, wy_hi, wy_lo, bz_hl, True, dark_col if first else None, *scratch, finish)


def kind_spec(shape, kind):
    return pl.BlockSpec((1,) + shape, lambda i: (kind,) + (0,) * len(shape))


def whole(*shape):
    return pl.BlockSpec(shape, lambda i: (0,) * len(shape))


def table_specs(kind):
    return [kind_spec((8, 256, 256), kind), kind_spec((8, 256, 256), kind), kind_spec((256, 256), kind)]


VOLUME = (XB, 128, 128)
FACES = (2, 8, 128, 128)
PACKS = (2, 4, 128, 128)
HALOS = [whole(*FACES), whole(2, 6, 128, 128)]


def ratio(first, estimate, observed, halos, tables, px):
    wy_hi, wy_lo, bz_hl, edges, dark_col = tables
    return pl.pallas_call(
        lambda *refs: ratio_kernel(first, *refs),
        grid=(1,),
        out_shape=[
            jax.ShapeDtypeStruct(VOLUME, F32),
            jax.ShapeDtypeStruct(FACES, BF),
            jax.ShapeDtypeStruct(PACKS, BF),
        ],
        in_specs=[SM, whole(*VOLUME), whole(*VOLUME), *HALOS, whole(128, 128), *table_specs(0), whole(8, 128, 256)],
        out_specs=[whole(*VOLUME), whole(*FACES), whole(*PACKS)],
        scratch_shapes=SCRATCH,
        compiler_params=params(44),
        name="ratio",
    )(px, estimate, observed, *halos, dark_col, wy_hi, wy_lo, bz_hl, edges)


def update_kernel(first, last, px, quotient, estimate, x_halo, y_halo, dark_col, wy_hi, wy_lo, bz_hl, edges, *refs):
    if last:
        coded, peak, woven, top, *scratch = refs
        top[...] = jnp.zeros_like(top)
    else:
        new, faces, packs, *scratch = refs

    def finish(k, results):
        values = []
        for s in range(8):
            x = k * 8 + s
            old = estimate[x]
            if first:
                old = old.astype(F32) + dark_col[...]
            value = old * results[s]
            if last:
                woven[pl.ds(x, 128, stride=XB), :] = value
                top[...] = jnp.maximum(top[...], value)
            else:
                new[x] = value
                values.append(value.astype(BF))
        if not last:
            store_edges(k, values, edges, faces, packs)

    blur_block(lambda x: quotient[x], x_halo, y_halo, px, wy_hi, wy_lo, bz_hl, False, None, *scratch, finish)
    if last:
        highest = jnp.max(top[...])
        scale = 2.0**15 / jnp.where(highest > 0.0, highest, 1.0)
        peak[...] = jnp.full((1, 128), highest, F32)

        def encode(i, carry):
            part = woven[pl.ds(pl.multiple_of(i * 256, 256), 256), :] * scale
            part = part * part
            part = part * part
            coded[pl.ds(i * 8, 8)] = (part * part).astype(BF).reshape(8, XB, 128)
            return carry

        lax.fori_loop(0, NZ // 8, encode, 0)


def update(first, last, quotient, estimate, halos, tables, px):
    wy_hi, wy_lo, bz_hl, edges, dark_col = tables
    if last:
        out_shape = [jax.ShapeDtypeStruct((NZ, XB, 128), BF), jax.ShapeDtypeStruct((1, 128), F32)]
        out_specs = [whole(NZ, XB, 128), whole(1, 128)]
        extra = [pltpu.VMEM((NZ * XB, 128), F32), pltpu.VMEM((128, 128), F32)]
    else:
        out_shape = [
            jax.ShapeDtypeStruct(VOLUME, F32),
            jax.ShapeDtypeStruct(FACES, BF),
            jax.ShapeDtypeStruct(PACKS, BF),
        ]
        out_specs = [whole(*VOLUME), whole(*FACES), whole(*PACKS)]
        extra = []
    return pl.pallas_call(
        lambda *refs: update_kernel(first, last, *refs),
        grid=(1,),
        out_shape=out_shape,
        in_specs=[SM, whole(*VOLUME), whole(*VOLUME), *HALOS, whole(128, 128), *table_specs(1), whole(8, 128, 256)],
        out_specs=out_specs,
        scratch_shapes=extra + SCRATCH,
        compiler_params=params(48),
        name="update",
    )(px, quotient, estimate, *halos, dark_col, wy_hi, wy_lo, bz_hl, edges)


def shards(raw_planes, slot_plane, shear_offsets, dark_level, profile_z, profile_x, profile_y):
    tables = make_tables(profile_z, profile_x, profile_y, dark_level)
    blocks, label_row = shear(slot_plane, shear_offsets, raw_planes)
    received, labels = scatter(blocks, label_row)
    observed, faces, packs = place(received, labels, tables[3])
    estimate = observed
    for iteration in range(ITERS):
        first, last = iteration == 0, iteration == ITERS - 1
        halos = exchange(faces, packs, 2)
        quotient, faces, packs = ratio(first, estimate, observed, halos, tables, profile_x)
        halos = exchange(faces, packs, 2)
        estimate, *rest = update(first, last, quotient, estimate, halos, tables, profile_x)
        if not last:
            faces, packs = rest
    coded, peaks = collect(estimate, rest[0])
    decoded = jnp.sqrt(jnp.sqrt(jnp.sqrt(coded.astype(F32)))).reshape(4, NB, XB, 128) * (peaks[None] * 2.0**-15)
    return decoded.reshape(4, NB * XB, 128)


def solution(mesh):
    in_specs = (P("gz", None, "gy"), P("gz"), P(), P(), P(), P(), P())
    out_specs = P("gz", None, "gy")
    return jax.shard_map(shards, mesh=mesh, in_specs=in_specs, out_specs=out_specs, check_vma=False)
```

time: 463 us -> 213 us (0.46)
  the two profiles are of different devices: /device:TPU:33 before, /device:TPU:23 now
where the time goes in v1:
time: 213 us; the launch traced here: 209 us
  Pallas kernels  201 us (94%)
  local copies, waits for them, and re-layouts  4.28 us (2%)
  other arithmetic  2.9 us (1%)
    pallas_call x1, Pallas kernels, scatter(): pl.pallas_call(scatter_kernel, out_shape=[jax.ShapeDtypeStruct((NB, 16, 1...  56.6 us
    pallas_call x4, Pallas kernels, exchange(): pl.pallas_call(halo_kernel, out_shape=[jax.ShapeDtypeStruct((2, 8, 128, 1...  56 us
    pallas_call x1, Pallas kernels, collect(): pl.pallas_call(collect_kernel, out_shape=[jax.ShapeDtypeStruct((4, NB * X...  32.4 us
    pallas_call x2, Pallas kernels, update(): pl.pallas_call(lambda *refs: update_kernel(first, last, *refs), grid=(1,)...  25.5 us
    pallas_call x2, Pallas kernels, ratio(): pl.pallas_call(lambda *refs: ratio_kernel(first, *refs), grid=(1,), out_s...  23 us

profile of v1, /device:TPU:23, one launch (start us, length us, event | category | flops | bytes accessed | tf_op | source)
XLA Modules:
  0.0 208.8 jit_solution(10297443814287300230)
XLA Ops:
  0.0 0.0 copy-start.5
  0.0 1.6 copy-done.5
  1.6 0.0 copy-start.10
  1.6 0.7 copy-done.10
  2.2 0.0 copy-start.11
  2.2 0.7 copy-done.11
  2.9 0.0 copy-start.6
  2.9 0.0 copy-start.7
  2.9 0.0 copy-start.8
  2.9 0.0 copy-start.9
  2.9 2.4 %shear.1 = (bf16[512,16,128]{2,1,0:T(8,128)(2,1)S(1)}, s32[1,128]{1,0:T(1,128)S(1)}) custom-call(s32[8]{0:T(128)S(1)} %copy-done.10, s32[128]{0:T(128)S(1)} %copy-done.11, bf16[8,1024,128]{2,1,0:T(8,128)(2,1)S(1)} %copy-done.5), custom_call_target="tpu_custom_call" | custom-call | tf_op jit(solution)/shard_map/shear/pallas_call | solution.py:134
  5.3 56.6 %scatter.1 = (bf16[32,16,16,128]{3,2,1,0:T(8,128)(2,1)S(1)}, s32[32,1,128]{2,1,0:T(1,128)S(1)}) custom-call(bf16[512,16,128]{2,1,0:T(8,128)(2,1)S(1)} %get-tuple-element.38.blocks, s32[1,128]{1,0:T(1,128)S(1)} %get-tuple-element.39.label_row), custom_call_target="tpu_custom_call" | custom-call | tf_op jit(solution)/shard_map/scatter/pallas_call | solution.py:211
  61.9 0.0 copy-done.6
  61.9 0.0 copy-done.7
  61.9 0.0 copy-done.8
  61.9 0.0 copy-done.9
  61.9 2.8 %tables.1 = (bf16[2,8,256,256]{3,2,1,0:T(8,128)(2,1)S(1)}, bf16[2,8,256,256]{3,2,1,0:T(8,128)(2,1)S(1)}, bf16[2,256,256]{2,1,0:T(8,128)(2,1)S(1)}, bf16[8,128,256]{2,1,0:T(8,128)(2,1)S(1)}, f32[128,128]{1,0:T(8,128)S(1)}) custom-call(f32[2,41]{1,0:T(2,128)S(1)} %copy-done.7, f32[2,15]{1,0:T(2,128)S(1)} %copy-done.6, f32[2,15]{1,0:T(2,128)S(1)} %copy-done.8, ...), custom_call_target="tpu_custom_call" | custom-call | tf_op jit(solution)/shard_map/tables/pallas_call | solution.py:91
  64.7 0.0 copy-start
  64.7 0.0 copy-start.2
  64.7 2.8 %place.1 = (bf16[32,128,128]{2,1,0:T(8,128)(2,1)S(1)}, bf16[2,8,128,128]{3,2,1,0:T(8,128)(2,1)S(1)}, bf16[2,4,128,128]{3,2,1,0:T(8,128)(2,1)S(1)}) custom-call(bf16[32,16,16,128]{3,2,1,0:T(8,128)(2,1)S(1)} %get-tuple-element.40.received, s32[32,1,128]{2,1,0:T(1,128)S(1)} %get-tuple-element.41.labels, bf16[8,128,256]{2,1,0:T(8,128)(2,1)S(1)} %get-tuple-element.42.edges.refs_9_), custom_call_target="tpu_custom_call" | custom-call | tf_op jit(solution)/shard_map/place/pallas_call | solution.py:389
  67.5 10.9 %halo.4 = (bf16[2,8,128,128]{3,2,1,0:T(8,128)(2,1)S(1)}, bf16[2,6,128,128]{3,2,1,0:T(8,128)(2,1)S(1)}) custom-call(bf16[2,8,128,128]{3,2,1,0:T(8,128)(2,1)S(1)} %get-tuple-element.44.faces, bf16[2,4,128,128]{3,2,1,0:T(8,128)(2,1)S(1)} %get-tuple-element.45.packs), custom_call_target="tpu_custom_call" | custom-call | tf_op jit(solution)/shard_map/halo/pallas_call | solution.py:325
  78.4 11.1 %ratio.2 = (f32[32,128,128]{2,1,0:T(8,128)S(1)}, bf16[2,8,128,128]{3,2,1,0:T(8,128)(2,1)S(1)}, bf16[2,4,128,128]{3,2,1,0:T(8,128)(2,1)S(1)}) custom-call(f32[2,15]{1,0:T(2,128)S(1)} %copy-done.6, bf16[32,128,128]{2,1,0:T(8,128)(2,1)S(1)} %get-tuple-element.43.refs_1_.refs_2_, bf16[32,128,128]{2,1,0:T(8,128)(2,1)S(1)} %get-tuple-element.43.refs_1_.refs_2_, ...), custom_call_target="tpu_custom_call" | custom-call | tf_op jit(solution)/shard_map/ratio/pallas_call | solution.py:524
  89.5 0.0 copy-done
  89.5 0.0 copy-done.2
  89.5 0.0 copy-start.4
  89.5 1.3 copy-done.4
  90.8 19.7 %halo.5 = (bf16[2,8,128,128]{3,2,1,0:T(8,128)(2,1)S(1)}, bf16[2,6,128,128]{3,2,1,0:T(8,128)(2,1)S(1)}) custom-call(bf16[2,8,128,128]{3,2,1,0:T(8,128)(2,1)S(1)} %get-tuple-element.53.faces, bf16[2,4,128,128]{3,2,1,0:T(8,128)(2,1)S(1)} %get-tuple-element.54.packs), custom_call_target="tpu_custom_call" | custom-call | tf_op jit(solution)/shard_map/halo/pallas_call | solution.py:325
  110.6 0.0 copy-start.1
  110.6 12.7 %update.2 = (f32[32,128,128]{2,1,0:T(8,128)S(1)}, bf16[2,8,128,128]{3,2,1,0:T(8,128)(2,1)S(1)}, bf16[2,4,128,128]{3,2,1,0:T(8,128)(2,1)S(1)}) custom-call(f32[2,15]{1,0:T(2,128)S(1)} %copy-done.6, f32[32,128,128]{2,1,0:T(8,128)} %copy-done.4, bf16[32,128,128]{2,1,0:T(8,128)(2,1)S(1)} %get-tuple-element.43.refs_1_.refs_2_, ...), custom_call_target="tpu_custom_call" | custom-call | tf_op jit(solution)/shard_map/update/pallas_call | solution.py:594
  123.3 0.0 copy-start.3
  123.3 12.9 %halo.6 = (bf16[2,8,128,128]{3,2,1,0:T(8,128)(2,1)S(1)}, bf16[2,6,128,128]{3,2,1,0:T(8,128)(2,1)S(1)}) custom-call(bf16[2,8,128,128]{3,2,1,0:T(8,128)(2,1)S(1)} %get-tuple-element.58.faces, bf16[2,4,128,128]{3,2,1,0:T(8,128)(2,1)S(1)} %get-tuple-element.59.packs), custom_call_target="tpu_custom_call" | custom-call | tf_op jit(solution)/shard_map/halo/pallas_call | solution.py:325
  136.2 0.0 copy-done.1
  136.2 11.9 %ratio.3 = (f32[32,128,128]{2,1,0:T(8,128)S(1)}, bf16[2,8,128,128]{3,2,1,0:T(8,128)(2,1)S(1)}, bf16[2,4,128,128]{3,2,1,0:T(8,128)(2,1)S(1)}) custom-call(f32[2,15]{1,0:T(2,128)S(1)} %copy-done.6, f32[32,128,128]{2,1,0:T(8,128)S(1)} %get-tuple-element.57.refs_1_.refs_2_, bf16[32,128,128]{2,1,0:T(8,128)(2,1)S(1)} %get-tuple-element.43.refs_1_.refs_2_, ...), custom_call_target="tpu_custom_call" | custom-call | tf_op jit(solution)/shard_map/ratio/pallas_call | solution.py:524
  148.1 0.0 copy-done.3
  148.1 12.6 %halo.7 = (bf16[2,8,128,128]{3,2,1,0:T(8,128)(2,1)S(1)}, bf16[2,6,128,128]{3,2,1,0:T(8,128)(2,1)S(1)}) custom-call(bf16[2,8,128,128]{3,2,1,0:T(8,128)(2,1)S(1)} %get-tuple-element.63.faces, bf16[2,4,128,128]{3,2,1,0:T(8,128)(2,1)S(1)} %get-tuple-element.64.packs), custom_call_target="tpu_custom_call" | custom-call | tf_op jit(solution)/shard_map/halo/pallas_call | solution.py:325
  160.7 12.8 %update.3 = (bf16[128,32,128]{2,1,0:T(8,128)(2,1)S(1)}, f32[1,128]{1,0:T(1,128)S(1)}) custom-call(f32[2,15]{1,0:T(2,128)S(1)} %copy-done.6, f32[32,128,128]{2,1,0:T(8,128)S(1)} %get-tuple-element.62.refs_1_, f32[32,128,128]{2,1,0:T(8,128)} %copy-done.3, bf16[2,8,128,128]{3,2,1,0:T(8,128)(2,1)S(1)} %get-tuple-element.65.refs_3_, ...), custom_call_target="tpu_custom_call" | custom-call | tf_op jit(solution)/shard_map/update/pallas_call | solution.py:594
  173.5 32.4 %collect.1 = (bf16[4,1024,128]{2,1,0:T(8,128)(2,1)S(1)}, f32[32,1,128]{2,1,0:T(1,128)S(1)}) custom-call(bf16[128,32,128]{2,1,0:T(8,128)(2,1)S(1)} %get-tuple-element.67.coded, f32[1,128]{1,0:T(1,128)S(1)} %get-tuple-element.68.peak), custom_call_target="tpu_custom_call" | custom-call | tf_op jit(solution)/shard_map/collect/pallas_call | solution.py:275
  205.9 2.9 %sqrt_multiply_fusion = f32[4,1024,128]{2,1,0:T(8,128)} fusion(bf16[4,1024,128]{2,1,0:T(8,128)(2,1)S(1)} %get-tuple-element.69, f32[1024,128]{1,0:T(8,128)S(1)} %bitcast.4), kind=kLoop, calls=%fused_computation | loop fusion | flops 1048576 | bytes 3670016 | tf_op jit(solution)/shard_map/mul | solution.py:621
  (2 shorter events, 0.1 us)
Async XLA Ops:
  0.0 1.6 copy-start.5
  1.6 0.7 copy-start.10
  2.2 0.7 copy-start.11
  2.9 59.0 %copy-start.6 = (f32[2,15]{1,0:T(2,128)S(1)}, f32[2,15]{1,0:T(2,128)}, u32[]{:S(2)}) copy-start(f32[2,15]{1,0:T(2,128)} %refs_0_.7) | copy-start | bytes 364
  2.9 59.0 %copy-start.7 = (f32[2,41]{1,0:T(2,128)S(1)}, f32[2,41]{1,0:T(2,128)}, u32[]{:S(2)}) copy-start(f32[2,41]{1,0:T(2,128)} %pz.1) | copy-start | bytes 988
  2.9 59.0 %copy-start.8 = (f32[2,15]{1,0:T(2,128)S(1)}, f32[2,15]{1,0:T(2,128)}, u32[]{:S(2)}) copy-start(f32[2,15]{1,0:T(2,128)} %py.1) | copy-start | bytes 364
  2.9 59.0 %copy-start.9 = (f32[128]{0:T(128)S(1)}, f32[128]{0:T(128)}, u32[]{:S(2)}) copy-start(f32[128]{0:T(128)} %param.10) | copy-start | bytes 1540
  64.7 24.8 %copy-start = (bf16[2,8,256,256]{3,2,1,0:T(8,128)(2,1)}, bf16[2,8,256,256]{3,2,1,0:T(8,128)(2,1)S(1)}, u32[]{:S(2)}) copy-start(bf16[2,8,256,256]{3,2,1,0:T(8,128)(2,1)S(1)} %get-tuple-element.49.refs_6_) | copy-start | bytes 6291460
  64.7 24.8 %copy-start.2 = (bf16[2,8,256,256]{3,2,1,0:T(8,128)(2,1)}, bf16[2,8,256,256]{3,2,1,0:T(8,128)(2,1)S(1)}, u32[]{:S(2)}) copy-start(bf16[2,8,256,256]{3,2,1,0:T(8,128)(2,1)S(1)} %get-tuple-element.50.refs_7_) | copy-start | bytes 6291460
  89.5 1.3 copy-start.4
  110.6 25.6 %copy-start.1 = (bf16[2,8,256,256]{3,2,1,0:T(8,128)(2,1)S(1)}, bf16[2,8,256,256]{3,2,1,0:T(8,128)(2,1)}, u32[]{:S(2)}) copy-start(bf16[2,8,256,256]{3,2,1,0:T(8,128)(2,1)} %copy-done) | copy-start | bytes 6291460
  123.3 24.8 %copy-start.3 = (f32[32,128,128]{2,1,0:T(8,128)}, f32[32,128,128]{2,1,0:T(8,128)S(1)}, u32[]{:S(2)}) copy-start(f32[32,128,128]{2,1,0:T(8,128)S(1)} %get-tuple-element.57.refs_1_.refs_2_) | copy-start | bytes 6291460

commit v2 on v1

v2 whole, which is shorter than its diff:
```python
import jax
import jax.numpy as jnp
from jax import lax
from jax.experimental import pallas as pl
from jax.experimental.pallas import tpu as pltpu
from jax.sharding import PartitionSpec as P

SHEAR = 256
ITERS = 2
NZ = 128
NB = 32
XB = 32
YB = 128
CAP = 8
TX = 15
TZ = 41
MESH = pl.DeviceIdType.MESH
BF = jnp.bfloat16
F32 = jnp.float32
I32 = jnp.int32
V = pl.BlockSpec(memory_space=pltpu.VMEM)
SM = pl.BlockSpec(memory_space=pltpu.SMEM)
ANY = pl.BlockSpec(memory_space=pl.ANY)


def params(mib, **kw):
    return pltpu.CompilerParams(vmem_limit_bytes=mib * 2**20, **kw)


def snake(g):
    high = lax.div(g, 8)
    y = lax.rem(lax.div(g, 2), 4)
    flip = lax.rem(high, 2)
    return high * 8 + (y + flip * (3 - 2 * y)) * 2 + lax.rem(g, 2)


def iota(shape, dim):
    return lax.broadcasted_iota(I32, shape, dim)


def dot(a, b):
    return jnp.dot(a, b, preferred_element_type=F32)


def split(v):
    hi = v.astype(BF)
    return hi, (v - hi.astype(F32)).astype(BF)


def toeplitz(profile, r, distance, extent, mirror):
    total = jnp.zeros(distance.shape, F32)
    for d in range(extent):
        total = jnp.where(distance == d, profile[r, extent - 1 - d if mirror else d], total)
    return total


def tables_kernel(pz, px, py, dark, wy_hi, wy_lo, bz_hl, edges, dark_col):
    for kind in range(2):
        mirror = kind == 0
        for r in range(2):
            lanes = pl.ds(r * 128, 128)
            row = iota((128, 128), 0)
            col = iota((128, 128), 1)
            hi, lo = split(toeplitz(py, r, row - col + 7, TX, mirror))
            for s in range(8):
                wy_hi[kind, s, 0:128, lanes] = hi
                wy_lo[kind, s, 0:128, lanes] = lo
            h = lax.rem(row, 16)
            source = jnp.where(h < 8, h - 7, h + 120)
            distance = jnp.where(lax.rem(h, 8) == 7, -1, source - col + 7)
            halo = toeplitz(py, r, distance, TX, mirror)
            for s in range(8):
                hi, lo = split(jnp.where(lax.div(row, 16) == s, halo, 0.0))
                wy_hi[kind, s, 128:256, lanes] = hi
                wy_lo[kind, s, 128:256, lanes] = lo
            hi, lo = split(toeplitz(pz, r, col - row + TZ // 2, TZ, mirror))
            bz_hl[kind, 0:128, lanes] = hi
            bz_hl[kind, 128:256, lanes] = lo
    row = iota((128, 128), 0)
    col = iota((128, 128), 1)
    for s in range(8):
        near = (col == s * 16 + 8 + row) & (row < 7)
        far = (col == s * 16 + row - 121) & (row >= 121)
        edges[s, :, 0:128] = jnp.where(near, 1.0, 0.0).astype(BF)
        edges[s, :, 128:256] = jnp.where(far, 1.0, 0.0).astype(BF)
    level = jnp.sum(jnp.where(row == col, dark[...], 0.0), axis=1, keepdims=True)
    dark_col[...] = jnp.broadcast_to(level, (128, 128))


def make_tables(profile_z, profile_x, profile_y, dark_level):
    return pl.pallas_call(
        tables_kernel,
        out_shape=[
            jax.ShapeDtypeStruct((2, 8, 256, 256), BF),
            jax.ShapeDtypeStruct((2, 8, 256, 256), BF),
            jax.ShapeDtypeStruct((2, 256, 256), BF),
            jax.ShapeDtypeStruct((8, 128, 256), BF),
            jax.ShapeDtypeStruct((128, 128), F32),
        ],
        in_specs=[SM, SM, SM, V],
        out_specs=[V] * 5,
        compiler_params=params(24),
        name="tables",
    )(profile_z, profile_x, profile_y, dark_level.reshape(1, 128))


def shear_kernel(slot, offsets, raw, blocks, label_row, padded, woven):
    columns = raw.shape[1]
    lane = lax.rem(iota((1, 128), 1), CAP)
    labels = jnp.zeros((1, 128), I32)
    for k in range(2):
        padded[k, 0:SHEAR] = jnp.zeros((SHEAR, 128), F32)
    for c in range(CAP):
        plane = slot[c]
        labels = jnp.where(lane == c, plane, labels)
        start = SHEAR - offsets[jnp.maximum(plane, 0)]
        k = c % 2
        for x in range(0, columns, 256):
            padded[k, SHEAR + x : SHEAR + x + 256] = raw[c, x : x + 256].astype(F32)
        for x in range(0, columns, 256):
            woven[pl.ds(x * CAP + c, 256, stride=CAP), :] = padded[k, pl.ds(start + x, 256), :]
    label_row[...] = labels

    def pack(i, carry):
        at = pl.ds(pl.multiple_of(i * 512, 512), 512)
        blocks[pl.ds(i * 32, 32)] = woven[at, :].reshape(32, 16, 128).astype(BF)
        return carry

    lax.fori_loop(0, columns * CAP // 512, pack, 0)


def shear(slot_plane, shear_offsets, raw):
    columns = raw.shape[1]
    return pl.pallas_call(
        shear_kernel,
        out_shape=[
            jax.ShapeDtypeStruct((columns // 2, 16, 128), BF),
            jax.ShapeDtypeStruct((1, 128), I32),
        ],
        in_specs=[SM, SM, V],
        out_specs=[V, V],
        scratch_shapes=[
            pltpu.VMEM((2, SHEAR + columns, 128), F32),
            pltpu.VMEM((columns * CAP, 128), F32),
        ],
        compiler_params=params(24),
        name="shear",
    )(slot_plane, shear_offsets, raw)


def greet_all(g, q):
    barrier = pltpu.get_barrier_semaphore()

    def hello(k, carry):
        pl.semaphore_signal(barrier, inc=1, device_id=(lax.rem(g + k, NB), q), device_id_type=MESH)
        return carry

    lax.fori_loop(1, NB, hello, 0)
    pl.semaphore_wait(barrier, NB - 1)


def scatter_kernel(blocks, label_row, received, labels, send, recv, send_small, recv_small, own):
    g = lax.axis_index("gz")
    q = lax.axis_index("gy")
    greet_all(g, q)

    def pair(k, target):
        block = snake(target)
        big = pltpu.make_async_remote_copy(
            src_ref=blocks.at[pl.ds(block * 16, 16)],
            dst_ref=received.at[g],
            send_sem=send.at[k],
            recv_sem=recv.at[k],
            device_id=(target, q),
            device_id_type=MESH,
        )
        small = pltpu.make_async_remote_copy(
            src_ref=label_row,
            dst_ref=labels.at[g],
            send_sem=send_small.at[k],
            recv_sem=recv_small.at[k],
            device_id=(target, q),
            device_id_type=MESH,
        )
        return big, small

    def start(k, carry):
        for copy in pair(k, lax.rem(g + k, NB)):
            copy.start()
        return carry

    lax.fori_loop(1, NB, start, 0)
    mine = (
        pltpu.make_async_copy(blocks.at[pl.ds(snake(g) * 16, 16)], received.at[g], own.at[0]),
        pltpu.make_async_copy(label_row, labels.at[g], own.at[1]),
    )
    for copy in mine:
        copy.start()
    for copy in mine:
        copy.wait()

    def finish(k, carry):
        for copy in pair(k, lax.rem(g + k, NB)):
            copy.wait()
        return carry

    lax.fori_loop(1, NB, finish, 0)


def scatter(blocks, label_row):
    return pl.pallas_call(
        scatter_kernel,
        out_shape=[
            jax.ShapeDtypeStruct((NB, 16, 16, 128), BF),
            jax.ShapeDtypeStruct((NB, 1, 128), I32),
        ],
        in_specs=[ANY, ANY],
        out_specs=[ANY, ANY],
        scratch_shapes=[pltpu.SemaphoreType.DMA((NB,))] * 4 + [pltpu.SemaphoreType.DMA((2,))],
        compiler_params=params(8, collective_id=0, has_side_effects=True),
        name="scatter",
    )(blocks, label_row)


def onehot_of(labels):
    plane = iota((128, 128), 0)
    lane = iota((128, 128), 1)
    spot = lax.div(iota((1, 128), 1), 16)
    parts = []
    for chunk in range(4):
        row = jnp.zeros((1, 128), I32)
        for j in range(8):
            row = jnp.where(spot == j, labels[chunk * 8 + j], row)
        parts.append(row == plane)
    parity = lax.rem(lax.div(lane, CAP), 2)
    return jnp.concatenate(
        [
            jnp.concatenate([jnp.where(hit & (parity == p), 1.0, 0.0).astype(BF) for hit in parts], axis=1)
            for p in range(2)
        ],
        axis=0,
    )


STEPS = 2 * ITERS
MOVES = 14


def solve_kernel(
    px, received, labels, dark_col, wy_hi, wy_lo, bz_hl, edges, out, peaks,
    observed, estimate, by_y, x_hi, x_lo, faces, packs, x_halo, y_halo, coded, peak, woven, top,
    send, recv, send_big, recv_big, send_small, recv_small, own,
):
    g = lax.axis_index("gz")
    q = lax.axis_index("gy")
    b = snake(g)
    count = lax.axis_size("gy")
    up, down = snake(lax.rem(b + 1, NB)), snake(lax.rem(b + NB - 1, NB))
    right, left = lax.rem(q + 1, count), lax.rem(q + count - 1, count)

    barrier = pltpu.get_barrier_semaphore()

    def hello(k, carry):
        pl.semaphore_signal(barrier, inc=1, device_id=(lax.rem(g + k, NB), q), device_id_type=MESH)
        return carry

    lax.fori_loop(1, NB, hello, 0)
    for device in [(d, e) for d in (down, g, up) for e in (left, right)]:
        pl.semaphore_signal(barrier, inc=1, device_id=device, device_id_type=MESH)
    pl.semaphore_wait(barrier, NB - 1 + 6)

    def move(i, n, src, dst, device):
        return pltpu.make_async_remote_copy(
            src_ref=src,
            dst_ref=dst,
            send_sem=send.at[i, n],
            recv_sem=recv.at[i, n],
            device_id=device,
            device_id_type=MESH,
        )

    def pack_moves(i, k):
        return [
            move(i, k, packs.at[i, 1, k], y_halo.at[i, 0, k + 1], (g, right)),
            move(i, 4 + k, packs.at[i, 0, k], y_halo.at[i, 1, k + 1], (g, left)),
        ]

    def face_down(i):
        return move(i, 8, faces.at[i, 0, pl.ds(0, 7)], x_halo.at[i, 1, pl.ds(0, 7)], (down, q))

    def face_up(i):
        return move(i, 9, faces.at[i, 1, pl.ds(1, 7)], x_halo.at[i, 0, pl.ds(1, 7)], (up, q))

    def first_corners(i):
        return [
            move(i, 10, packs.at[i, 1, 0], y_halo.at[i, 0, 5], (down, right)),
            move(i, 11, packs.at[i, 0, 0], y_halo.at[i, 1, 5], (down, left)),
        ]

    def last_corners(i):
        return [
            move(i, 12, packs.at[i, 1, 3], y_halo.at[i, 0, 0], (up, right)),
            move(i, 13, packs.at[i, 0, 3], y_halo.at[i, 1, 0], (up, left)),
        ]

    def all_moves(i):
        return [m for k in range(4) for m in pack_moves(i, k)] + [face_down(i), face_up(i)] + first_corners(i) + last_corners(i)

    def emit(i, k, values):
        @pl.when(k == 0)
        def _():
            for s in range(8):
                faces[i, 0, s] = values[s]
            face_down(i).start()

        @pl.when(k == 3)
        def _():
            for s in range(8):
                faces[i, 1, s] = values[s]
            face_up(i).start()

        total = dot(jnp.concatenate(values, axis=1), edges[...].reshape(1024, 256))
        packs[i, 0, k] = total[:, 0:128].astype(BF)
        packs[i, 1, k] = total[:, 128:256].astype(BF)

        @pl.when(k == 0)
        def _():
            for m in first_corners(i):
                m.start()

        @pl.when(k == 3)
        def _():
            for m in last_corners(i):
                m.start()

        for m in pack_moves(i, k):
            m.start()

    def along_y(at, values, kind):
        pairs = [split(v) for v in values]
        hi = jnp.concatenate([p[0] for p in pairs], axis=0)
        lo = jnp.concatenate([p[1] for p in pairs], axis=0)
        upper = wy_hi[kind, 0, 0:128]
        total = dot(jnp.concatenate([hi, lo], axis=1), jnp.concatenate([upper, upper], axis=0))
        total += dot(hi, wy_lo[kind, 0, 0:128])
        for s in range(len(values)):
            by_y[at + s, 0:128] = total[s * 128 : s * 128 + 128, 0:128]
            by_y[at + s, 128:256] = total[s * 128 : s * 128 + 128, 128:256]

    lane = lax.rem(iota((128, 128), 1), 16)
    outside_y = ((lane < 8) & (q == 0)) | ((lane >= 8) & (q == count - 1))

    def add_halo(i, group, members, kind, keep):
        halo = y_halo[i, 0, group].astype(F32) + y_halo[i, 1, group].astype(F32)
        if i == 0:
            halo += dark_col[...]
        halo = jnp.where(outside_y, 0.0, halo)
        if keep is not None:
            halo = jnp.where(keep, halo, 0.0)
        hi, lo = split(halo)
        both = jnp.concatenate([hi, lo], axis=1)
        for s in members:
            upper = wy_hi[kind, s, 128:256]
            if i == 0:
                total = dot(both, jnp.concatenate([upper, upper], axis=0))
            else:
                total = dot(hi, upper)
            total += dot(hi, wy_lo[kind, s, 128:256])
            at = group * 8 + s
            by_y[at, 0:128] += total[:, 0:128]
            by_y[at, 128:256] += total[:, 128:256]

    def along_x(mirror, spans):
        def tile(t, carry):
            for r in range(2):
                rows = pl.ds(pl.multiple_of(r * 128 + t * 16, 16), 16)
                for x, n in spans:
                    total = jnp.zeros((n, 16, 128), F32)
                    for j in range(TX):
                        total += px[r, TX - 1 - j if mirror else j] * by_y[x + 1 + j : x + 1 + j + n, rows, :]
                    hi, lo = split(total)
                    x_hi[x : x + n, rows, :] = hi
                    x_lo[x : x + n, rows, :] = lo
            return carry

        lax.fori_loop(0, 8, tile, 0)

    def along_z(k, kind):
        results = []
        for j in range(0, 8, 2):
            x = k * 8 + j
            hi = jnp.concatenate([x_hi[x], x_hi[x + 1]], axis=1)
            lo = jnp.concatenate([x_lo[x], x_lo[x + 1]], axis=1)
            both = dot(bz_hl[kind], hi)
            total = both[0:128] + both[128:256] + dot(bz_hl[kind, 0:128], lo)
            results += [total[:, 0:128], total[:, 128:256]]
        return results

    def in_order(j):
        return jnp.where(j == 0, 0, jnp.where(j == 1, 3, j - 1))

    onehot = onehot_of(labels)

    def start_group(j, carry):
        k = in_order(j)
        values = []
        for p in range(4):
            both = dot(onehot, received[:, k * 4 + p].reshape(NB * 16, 128))
            values += [both[0:128], both[128:256]]
        for s in range(8):
            observed[k * 8 + s] = values[s].astype(BF)
        emit(0, k, [v.astype(BF) for v in values])
        values = [v + dark_col[...] for v in values]
        for s in range(8):
            estimate[k * 8 + s] = values[s]
        along_y(8 + k * 8, values, 0)
        return carry

    lax.fori_loop(0, 4, start_group, 0)
    top[...] = jnp.zeros_like(top)

    for i in range(STEPS):
        kind = i % 2
        last = i == STEPS - 1
        moves = all_moves(i)
        for m in moves[0:8]:
            m.wait_recv()

        def main_halo(k, carry, i=i, kind=kind):
            add_halo(i, k + 1, range(8), kind, None)
            return carry

        lax.fori_loop(0, 4, main_halo, 0)
        along_x(kind == 0, [(7, 9), (16, 9)])
        for m in moves[8:]:
            m.wait_recv()
        for side, group, members, keep in ((0, 0, range(1, 8), b > 0), (1, 5, range(0, 7), b < NB - 1)):
            values = []
            for s in members:
                v = x_halo[i, side, s].astype(F32)
                if i == 0:
                    v += dark_col[...]
                values.append(jnp.where(keep, v, 0.0))
            along_y(group * 8 + members[0], values, kind)
            add_halo(i, group, members, kind, keep)
        along_x(kind == 0, [(0, 7), (25, 7)])

        def end_group(j, carry, i=i, kind=kind, last=last):
            k = in_order(j)
            results = along_z(k, kind)
            values = []
            for s in range(8):
                x = k * 8 + s
                if kind == 0:
                    value = observed[x].astype(F32) / (results[s] + dark_col[...])
                else:
                    value = estimate[x] * results[s]
                    if last:
                        woven[pl.ds(x, 128, stride=XB), :] = value
                        top[...] = jnp.maximum(top[...], value)
                    else:
                        estimate[x] = value
                values.append(value)
            if not last:
                emit(i + 1, k, [v.astype(BF) for v in values])
                along_y(8 + k * 8, values, 1 - kind)
            return carry

        lax.fori_loop(0, 4, end_group, 0)

    highest = jnp.max(top[...])
    scale = 2.0**15 / jnp.where(highest > 0.0, highest, 1.0)
    peak[...] = jnp.full((1, 128), highest, F32)

    def encode(n, carry):
        part = woven[pl.ds(pl.multiple_of(n * 256, 256), 256), :] * scale
        part = part * part
        part = part * part
        coded[pl.ds(n * 8, 8)] = (part * part).astype(BF).reshape(8, XB, 128)
        return carry

    lax.fori_loop(0, NZ // 8, encode, 0)
    rows = pl.ds(pl.multiple_of(b * XB, XB), XB)

    def pair(k, target):
        big = pltpu.make_async_remote_copy(
            src_ref=coded.at[pl.ds(target * 4, 4)],
            dst_ref=out.at[:, rows, :],
            send_sem=send_big.at[k],
            recv_sem=recv_big.at[k],
            device_id=(target, q),
            device_id_type=MESH,
        )
        small = pltpu.make_async_remote_copy(
            src_ref=peak,
            dst_ref=peaks.at[b],
            send_sem=send_small.at[k],
            recv_sem=recv_small.at[k],
            device_id=(target, q),
            device_id_type=MESH,
        )
        return big, small

    def start(k, carry):
        for copy in pair(k, lax.rem(g + k, NB)):
            copy.start()
        return carry

    lax.fori_loop(1, NB, start, 0)
    mine = (
        pltpu.make_async_copy(coded.at[pl.ds(g * 4, 4)], out.at[:, rows, :], own.at[0]),
        pltpu.make_async_copy(peak, peaks.at[b], own.at[1]),
    )
    for copy in mine:
        copy.start()
    for i in range(STEPS):
        for m in all_moves(i):
            m.wait_send()
    for copy in mine:
        copy.wait()

    def finish(k, carry):
        for copy in pair(k, lax.rem(g + k, NB)):
            copy.wait()
        return carry

    lax.fori_loop(1, NB, finish, 0)


def solve(received, labels, tables, px):
    wy_hi, wy_lo, bz_hl, edges, dark_col = tables
    dma = pltpu.SemaphoreType.DMA
    return pl.pallas_call(
        solve_kernel,
        out_shape=[
            jax.ShapeDtypeStruct((4, NB * XB, 128), BF),
            jax.ShapeDtypeStruct((NB, 1, 128), F32),
        ],
        in_specs=[SM] + [V] * 7,
        out_specs=[ANY, ANY],
        scratch_shapes=[
            pltpu.VMEM((XB, 128, 128), BF),
            pltpu.VMEM((XB, 128, 128), F32),
            pltpu.VMEM((48, 256, 128), F32),
            pltpu.VMEM((XB, 256, 128), BF),
            pltpu.VMEM((XB, 256, 128), BF),
            pltpu.VMEM((STEPS, 2, 8, 128, 128), BF),
            pltpu.VMEM((STEPS, 2, 4, 128, 128), BF),
            pltpu.VMEM((STEPS, 2, 8, 128, 128), BF),
            pltpu.VMEM((STEPS, 2, 6, 128, 128), BF),
            pltpu.VMEM((NZ, XB, 128), BF),
            pltpu.VMEM((1, 128), F32),
            pltpu.VMEM((NZ * XB, 128), F32),
            pltpu.VMEM((128, 128), F32),
            dma((STEPS, MOVES)),
            dma((STEPS, MOVES)),
            dma((NB,)),
            dma((NB,)),
            dma((NB,)),
            dma((NB,)),
            dma((2,)),
        ],
        compiler_params=params(44, collective_id=1, has_side_effects=True),
        name="solve",
    )(px, received, labels, dark_col, wy_hi, wy_lo, bz_hl, edges)


def shards(raw_planes, slot_plane, shear_offsets, dark_level, profile_z, profile_x, profile_y):
    tables = make_tables(profile_z, profile_x, profile_y, dark_level)
    blocks, label_row = shear(slot_plane, shear_offsets, raw_planes)
    received, labels = scatter(blocks, label_row)
    coded, peaks = solve(received, labels, tables, profile_x)
    decoded = jnp.sqrt(jnp.sqrt(jnp.sqrt(coded.astype(F32)))).reshape(4, NB, XB, 128) * (peaks[None] * 2.0**-15)
    return decoded.reshape(4, NB * XB, 128)


def solution(mesh):
    in_specs = (P("gz", None, "gy"), P("gz"), P(), P(), P(), P(), P())
    out_specs = P("gz", None, "gy")
    return jax.shard_map(shards, mesh=mesh, in_specs=in_specs, out_specs=out_specs, check_vma=False)
```

time: 213 us -> 178 us (0.84); the launches traced: 209 us -> 176 us
  Pallas kernels: 201 us -> 171 us
    pallas_call x10 -> x1, Pallas kernels: 140 us -> 109 us  [solve(): pl.pallas_call(solve_kernel, out_shape=[jax.ShapeDtypeStruct((4, NB * XB,...]
where the time goes in v2:
time: 178 us; the launch traced here: 176 us
  Pallas kernels  171 us (96%)
  local copies, waits for them, and re-layouts  2.95 us (2%)
  other arithmetic  2.9 us (2%)
    pallas_call x1, Pallas kernels, solve(): pl.pallas_call(solve_kernel, out_shape=[jax.ShapeDtypeStruct((4, NB * XB,...  109 us
    pallas_call x1, Pallas kernels, scatter(): pl.pallas_call(scatter_kernel, out_shape=[jax.ShapeDtypeStruct((NB, 16, 1...  56.6 us

profile of v2, /device:TPU:23, one launch (start us, length us, event | category | flops | bytes accessed | tf_op | source)
XLA Modules:
  0.0 176.5 jit_solution(9615797998733902805)
XLA Ops:
  0.0 0.0 copy-start
  0.0 1.6 copy-done
  1.6 0.0 copy-start.5
  1.6 0.7 copy-done.5
  2.2 0.0 copy-start.6
  2.2 0.7 copy-done.6
  2.9 0.0 copy-start.1
  2.9 0.0 copy-start.2
  2.9 0.0 copy-start.3
  2.9 0.0 copy-start.4
  2.9 2.4 %shear.1 = (bf16[512,16,128]{2,1,0:T(8,128)(2,1)S(1)}, s32[1,128]{1,0:T(1,128)S(1)}) custom-call(s32[8]{0:T(128)S(1)} %copy-done.5, s32[128]{0:T(128)S(1)} %copy-done.6, bf16[8,1024,128]{2,1,0:T(8,128)(2,1)S(1)} %copy-done), custom_call_target="tpu_custom_call" | custom-call | tf_op jit(solution)/shard_map/shear/pallas_call | solution.py:134
  5.3 56.6 %scatter.1 = (bf16[32,16,16,128]{3,2,1,0:T(8,128)(2,1)S(1)}, s32[32,1,128]{2,1,0:T(1,128)S(1)}) custom-call(bf16[512,16,128]{2,1,0:T(8,128)(2,1)S(1)} %get-tuple-element.16.blocks, s32[1,128]{1,0:T(1,128)S(1)} %get-tuple-element.17.label_row), custom_call_target="tpu_custom_call" | custom-call | tf_op jit(solution)/shard_map/scatter/pallas_call | solution.py:211
  61.9 0.0 copy-done.1
  61.9 0.0 copy-done.2
  61.9 0.0 copy-done.3
  62.0 0.0 copy-done.4
  62.0 2.8 %tables.1 = (bf16[2,8,256,256]{3,2,1,0:T(8,128)(2,1)S(1)}, bf16[2,8,256,256]{3,2,1,0:T(8,128)(2,1)S(1)}, bf16[2,256,256]{2,1,0:T(8,128)(2,1)S(1)}, bf16[8,128,256]{2,1,0:T(8,128)(2,1)S(1)}, f32[128,128]{1,0:T(8,128)S(1)}) custom-call(f32[2,41]{1,0:T(2,128)S(1)} %copy-done.2, f32[2,15]{1,0:T(2,128)S(1)} %copy-done.1, f32[2,15]{1,0:T(2,128)S(1)} %copy-done.3, ...), custom_call_target="tpu_custom_call" | custom-call | tf_op jit(solution)/shard_map/tables/pallas_call | solution.py:91
  64.7 108.8 %solve.1 = (bf16[4,1024,128]{2,1,0:T(8,128)(2,1)S(1)}, f32[32,1,128]{2,1,0:T(1,128)S(1)}) custom-call(f32[2,15]{1,0:T(2,128)S(1)} %copy-done.1, bf16[32,16,16,128]{3,2,1,0:T(8,128)(2,1)S(1)} %get-tuple-element.18.received, s32[32,1,128]{2,1,0:T(1,128)S(1)} %get-tuple-element.19.labels, f32[128,128]{1,0:T(8,128)S(1)} %get-tuple-element.20.dark_col, ...), custom_call_target="tpu_custom_call" | custom-call | tf_op jit(solution)/shard_map/solve/pallas_call | solution.py:533
  173.6 2.9 %sqrt_multiply_fusion = f32[4,1024,128]{2,1,0:T(8,128)} fusion(bf16[4,1024,128]{2,1,0:T(8,128)(2,1)S(1)} %get-tuple-element.25, f32[1024,128]{1,0:T(8,128)S(1)} %bitcast.4), kind=kLoop, calls=%fused_computation | loop fusion | flops 1048576 | bytes 3670016 | tf_op jit(solution)/shard_map/mul | solution.py:573
  (2 shorter events, 0.1 us)
Async XLA Ops:
  0.0 1.6 copy-start
  1.6 0.7 copy-start.5
  2.2 0.7 copy-start.6
  2.9 59.0 %copy-start.1 = (f32[2,15]{1,0:T(2,128)S(1)}, f32[2,15]{1,0:T(2,128)}, u32[]{:S(2)}) copy-start(f32[2,15]{1,0:T(2,128)} %px.3) | copy-start | bytes 364
  2.9 59.0 %copy-start.2 = (f32[2,41]{1,0:T(2,128)S(1)}, f32[2,41]{1,0:T(2,128)}, u32[]{:S(2)}) copy-start(f32[2,41]{1,0:T(2,128)} %pz.1) | copy-start | bytes 988
  2.9 59.0 %copy-start.3 = (f32[2,15]{1,0:T(2,128)S(1)}, f32[2,15]{1,0:T(2,128)}, u32[]{:S(2)}) copy-start(f32[2,15]{1,0:T(2,128)} %py.1) | copy-start | bytes 364
  2.9 59.0 %copy-start.4 = (f32[128]{0:T(128)S(1)}, f32[128]{0:T(128)}, u32[]{:S(2)}) copy-start(f32[128]{0:T(128)} %param.10) | copy-start | bytes 1540

commit v3 on v2

v3 whole, which is shorter than its diff:
```python
import jax
import jax.numpy as jnp
from jax import lax
from jax.experimental import pallas as pl
from jax.experimental.pallas import tpu as pltpu
from jax.sharding import PartitionSpec as P

SHEAR = 256
ITERS = 2
NZ = 128
NB = 32
XB = 32
YB = 128
CAP = 8
TX = 15
TZ = 41
MESH = pl.DeviceIdType.MESH
BF = jnp.bfloat16
F32 = jnp.float32
I32 = jnp.int32
V = pl.BlockSpec(memory_space=pltpu.VMEM)
SM = pl.BlockSpec(memory_space=pltpu.SMEM)
ANY = pl.BlockSpec(memory_space=pl.ANY)


def params(mib, **kw):
    return pltpu.CompilerParams(vmem_limit_bytes=mib * 2**20, **kw)


def snake(g):
    high = lax.div(g, 8)
    y = lax.rem(lax.div(g, 2), 4)
    flip = lax.rem(high, 2)
    return high * 8 + (y + flip * (3 - 2 * y)) * 2 + lax.rem(g, 2)


def iota(shape, dim):
    return lax.broadcasted_iota(I32, shape, dim)


def dot(a, b):
    return jnp.dot(a, b, preferred_element_type=F32)


def split(v):
    hi = v.astype(BF)
    return hi, (v - hi.astype(F32)).astype(BF)


def toeplitz(profile, r, distance, extent, mirror):
    total = jnp.zeros(distance.shape, F32)
    for d in range(extent):
        total = jnp.where(distance == d, profile[r, extent - 1 - d if mirror else d], total)
    return total


def fill_tables(pz, py, dark, wy, wh, spread, bz_hl, dark_col, dark_pack):
    row = iota((128, 128), 0)
    col = iota((128, 128), 1)
    level = jnp.sum(jnp.where(row == col, dark[...], 0.0), axis=1, keepdims=True)
    dark_col[...] = jnp.broadcast_to(level, (128, 128))
    tile = jnp.zeros((16, 128), F32)
    for n in range(8):
        tile = jnp.where(lax.div(iota((16, 128), 1), 16) == n, dark_col[n * 16 : n * 16 + 16], tile)
    for n in range(8):
        dark_pack[n * 16 : n * 16 + 16] = tile
        lane = lax.rem(n * 16 + col, 128)
        spread[n] = jnp.where((row == lane) & ((col < 7) | (col >= 121)), 1.0, 0.0).astype(BF)
    for kind in range(2):
        mirror = kind == 0
        for r in range(2):
            lanes = pl.ds(r * 128, 128)
            hi, lo = split(toeplitz(py, r, row - col + 7, TX, mirror))
            wy[kind, 0:128, lanes] = hi
            wy[kind, 128:256, lanes] = hi
            wy[kind, 256:384, lanes] = lo
            h = lax.rem(row, 16)
            delta = lax.rem(col - (row - h) + 192, 128) - 64
            distance = h - 1 - delta
            near = (h > 0) & (h < 8) & (delta >= 0) & (delta < 7)
            far = (h > 7) & (h < 15) & (delta < 0) & (delta > -8)
            hi, lo = split(toeplitz(py, r, jnp.where(near | far, distance, -1), TX, mirror))
            wh[kind, 0:128, lanes] = hi
            wh[kind, 128:256, lanes] = lo
            hi, lo = split(toeplitz(pz, r, col - row + TZ // 2, TZ, mirror))
            bz_hl[kind, 0:128, lanes] = hi
            bz_hl[kind, 128:256, lanes] = lo


def onehot_of(labels):
    plane = iota((128, 128), 0)
    lane = iota((128, 128), 1)
    spot = lax.div(iota((1, 128), 1), 16)
    parts = []
    for chunk in range(4):
        row = jnp.zeros((1, 128), I32)
        for j in range(8):
            row = jnp.where(spot == j, labels[chunk * 8 + j], row)
        parts.append(row == plane)
    parity = lax.rem(lax.div(lane, CAP), 2)
    return jnp.concatenate(
        [
            jnp.concatenate([jnp.where(hit & (parity == p), 1.0, 0.0).astype(BF) for hit in parts], axis=1)
            for p in range(2)
        ],
        axis=0,
    )


STEPS = 2 * ITERS
MOVES = 14
WIDE = XB + TX - 1
ROWS = 256


def whole_kernel(
    slot, offsets, pz, px, py, raw_hbm, dark, out, peaks,
    raw, padded, woven, blocks, label_row, received, labels, wy, wh, spread, bz_hl, dark_col, dark_pack,
    observed, estimate, e_hi, e_lo, by_a, by_b, by_x, y_rim, x_rim, x_hi, x_lo, faces, packs, x_halo, y_halo, coded, peak, final, top,
    load, send_raw, recv_raw, send_label, recv_label, send, recv, send_big, recv_big, send_small, recv_small, own,
):
    g = lax.axis_index("gz")
    q = lax.axis_index("gy")
    b = snake(g)
    count = lax.axis_size("gy")
    up, down = snake(lax.rem(b + 1, NB)), snake(lax.rem(b + NB - 1, NB))
    right, left = lax.rem(q + 1, count), lax.rem(q + count - 1, count)

    for c in range(CAP):
        pltpu.make_async_copy(raw_hbm.at[c], raw.at[c], load.at[c]).start()
    barrier = pltpu.get_barrier_semaphore()

    def hello(k, carry):
        pl.semaphore_signal(barrier, inc=1, device_id=(lax.rem(g + k, NB), q), device_id_type=MESH)
        return carry

    lax.fori_loop(1, NB, hello, 0)
    for device in [(d, e) for d in (down, g, up) for e in (left, right)]:
        pl.semaphore_signal(barrier, inc=1, device_id=device, device_id_type=MESH)


    label_lane = lax.rem(iota((1, 128), 1), CAP)
    row = jnp.zeros((1, 128), I32)
    for c in range(CAP):
        row = jnp.where(label_lane == c, slot[c], row)
    label_row[...] = row
    for c in range(CAP):
        padded[c, 0:SHEAR] = jnp.zeros((SHEAR, 128), F32)
    for c in range(CAP):
        pltpu.make_async_copy(raw_hbm.at[c], raw.at[c], load.at[c]).wait()

        def widen(n, carry, c=c):
            padded[c, pl.ds(pl.multiple_of(SHEAR + n * ROWS, ROWS), ROWS)] = raw[
                c, pl.ds(pl.multiple_of(n * ROWS, ROWS), ROWS)
            ].astype(F32)
            return carry

        lax.fori_loop(0, NB * XB // ROWS, widen, 0)
    pl.semaphore_wait(barrier, NB - 1 + 6)

    def block_to(target):
        return pltpu.make_async_remote_copy(
            src_ref=blocks.at[pl.ds(snake(target) * 16, 16)],
            dst_ref=received.at[g],
            send_sem=send_raw.at[target],
            recv_sem=recv_raw.at[g],
            device_id=(target, q),
            device_id_type=MESH,
        )

    def label_to(target):
        return pltpu.make_async_remote_copy(
            src_ref=label_row,
            dst_ref=labels.at[g],
            send_sem=send_label.at[target],
            recv_sem=recv_label.at[g],
            device_id=(target, q),
            device_id_type=MESH,
        )

    def block_from(source):
        return pltpu.make_async_remote_copy(
            src_ref=blocks.at[pl.ds(0, 16)],
            dst_ref=received.at[source],
            send_sem=send_raw.at[source],
            recv_sem=recv_raw.at[source],
            device_id=(source, q),
            device_id_type=MESH,
        )

    def label_from(source):
        return pltpu.make_async_remote_copy(
            src_ref=label_row,
            dst_ref=labels.at[source],
            send_sem=send_label.at[source],
            recv_sem=recv_label.at[source],
            device_id=(source, q),
            device_id_type=MESH,
        )

    def turn(n):
        return jnp.where(n == 0, 1, jnp.where(n == 1, 3, jnp.where(n == 2, 2, 0)))

    def shear_rows(n, carry):
        part = lax.rem(lax.div(g, 8) + turn(n), 4)
        x = part * ROWS
        for c in range(CAP):
            start = SHEAR - offsets[jnp.maximum(slot[c], 0)] + x
            woven[pl.ds(c, ROWS, stride=CAP), :] = padded[c, pl.ds(start, ROWS), :]
        for m in range(0, ROWS // 2, 32):
            at = pl.ds(pl.multiple_of(part * (ROWS // 2) + m, 32), 32)
            blocks[at] = woven[m * 16 : m * 16 + 512, :].reshape(32, 16, 128).astype(BF)

        def start_one(m, carry):
            target = snake(part * 8 + m)

            @pl.when(target != g)
            def _():
                block_to(target).start()
                label_to(target).start()

            return carry

        lax.fori_loop(0, 8, start_one, 0)
        return carry

    lax.fori_loop(0, NB * XB // ROWS, shear_rows, 0)
    mine = (
        pltpu.make_async_copy(blocks.at[pl.ds(b * 16, 16)], received.at[g], own.at[0]),
        pltpu.make_async_copy(label_row, labels.at[g], own.at[1]),
    )
    for copy in mine:
        copy.start()
    fill_tables(pz, py, dark, wy, wh, spread, bz_hl, dark_col, dark_pack)
    top[...] = jnp.zeros_like(top)
    for copy in mine:
        copy.wait()

    def arrive(k, carry):
        source = lax.rem(g + k, NB)
        block_from(source).wait_recv()
        label_from(source).wait_recv()
        return carry

    lax.fori_loop(1, NB, arrive, 0)


    def move(i, n, src, dst, device):
        return pltpu.make_async_remote_copy(
            src_ref=src,
            dst_ref=dst,
            send_sem=send.at[i, n],
            recv_sem=recv.at[i, n],
            device_id=device,
            device_id_type=MESH,
        )

    def pack_moves(i, k):
        return [
            move(i, k, packs.at[i, k], y_halo.at[i, 0, k + 1], (g, right)),
            move(i, 4 + k, packs.at[i, k], y_halo.at[i, 1, k + 1], (g, left)),
        ]

    def face_down(i):
        return move(i, 8, faces.at[i, 0, pl.ds(0, 7)], x_halo.at[i, 1, pl.ds(0, 7)], (down, q))

    def face_up(i):
        return move(i, 9, faces.at[i, 1, pl.ds(1, 7)], x_halo.at[i, 0, pl.ds(1, 7)], (up, q))

    def first_corners(i):
        return [
            move(i, 10, packs.at[i, 0, pl.ds(0, 112)], y_halo.at[i, 0, 5, pl.ds(0, 112)], (down, right)),
            move(i, 11, packs.at[i, 0, pl.ds(0, 112)], y_halo.at[i, 1, 5, pl.ds(0, 112)], (down, left)),
        ]

    def last_corners(i):
        return [
            move(i, 12, packs.at[i, 3, pl.ds(16, 112)], y_halo.at[i, 0, 0, pl.ds(16, 112)], (up, right)),
            move(i, 13, packs.at[i, 3, pl.ds(16, 112)], y_halo.at[i, 1, 0, pl.ds(16, 112)], (up, left)),
        ]

    def all_moves(i):
        moves = [m for k in range(4) for m in pack_moves(i, k)]
        return moves + [face_down(i), face_up(i)] + first_corners(i) + last_corners(i)

    chunk_of_lane = lax.div(iota((16, 128), 1), 16)

    def emit(i, k, values):
        @pl.when(k == 0)
        def _():
            for s in range(8):
                faces[i, 0, s] = values[s].astype(BF)
            face_down(i).start()

        @pl.when(k == 3)
        def _():
            for s in range(8):
                faces[i, 1, s] = values[s].astype(BF)
            face_up(i).start()

        for c in range(8):
            tile = jnp.zeros((16, 128), F32)
            for n in range(8):
                turned = pltpu.roll(values[c][n * 16 : n * 16 + 16], (n * 16 + 8) % 128, 1)
                tile = jnp.where(chunk_of_lane == n, turned, tile)
            packs[i, k, c * 16 : c * 16 + 16] = tile.astype(BF)
        for m in pack_moves(i, k):
            m.start()

    def emit_corners(i):
        for m in first_corners(i) + last_corners(i):
            m.start()

    lane = iota((128, 128), 1)
    lane16 = lax.rem(lane, 16)
    outside_y = ((lane16 < 8) & (q == 0)) | ((lane16 >= 8) & (q == count - 1))

    def rim_y(i, group, kind, keep):
        halo = jnp.where(lane16 < 8, y_halo[i, 0, group].astype(F32), y_halo[i, 1, group].astype(F32))
        if i == 0:
            halo += dark_pack[...]
        halo = jnp.where(outside_y, 0.0, halo)
        if keep is not None:
            halo = jnp.where(keep, halo, 0.0)
        halo = halo.astype(BF)
        total = dot(jnp.concatenate([halo, halo], axis=1), wh[kind])
        for r in range(2):
            y_rim[r, pl.ds(group * 8, 8)] = total[:, r * 128 : r * 128 + 128].reshape(8, 16, 128)

    def rim_x(mirror):
        for r in range(2):
            for x in range(0, XB, 8):
                total = px[r, TX - 1 if mirror else 0] * y_rim[r, x + 1 : x + 9]
                for j in range(1, TX):
                    total += px[r, TX - 1 - j if mirror else j] * y_rim[r, x + 1 + j : x + 9 + j]
                hi, lo = split(total)
                x_rim[r, x : x + 8, :, 0:128] = hi
                x_rim[r, x : x + 8, :, 128:256] = lo

    def add_rim(n, carry):
        place = jnp.concatenate([spread[2 * n], spread[2 * n + 1]], axis=1)
        for r in range(2):
            rim = x_rim[r].reshape(XB * 16, 256)
            added = dot(rim, jnp.concatenate([place, place], axis=0))
            for half in range(2):
                rows = pl.ds(pl.multiple_of(r * 128 + n * 32 + half * 16, 16), 16)
                part = added[:, half * 128 : half * 128 + 128].reshape(XB, 16, 128)
                hi, lo = split(by_x[:, rows, :] + part)
                x_hi[:, rows, :] = hi
                x_lo[:, rows, :] = lo
        return carry


    def y_piece(t, h, into, kind, first, n):
        rows = pl.ds(pl.multiple_of(t * 16, 16), 16)
        at = pl.ds(pl.multiple_of(h * 16, 16), 16)
        hi, lo = (e[first : first + n, rows, :].reshape(n * 16, 128) for e in (e_hi, e_lo))
        total = dot(jnp.concatenate([hi, lo, hi], axis=1), wy[kind])
        for r in range(2):
            into[r, first : first + n, at] = total[:, r * 128 : r * 128 + 128].reshape(n, 16, 128)

    def x_piece(t, h, source, mirror, first, n):
        at = pl.ds(pl.multiple_of(h * 16, 16), 16)
        for r in range(2):
            total = px[r, TX - 1 if mirror else 0] * source[r, first : first + n, at]
            for j in range(1, TX):
                total += px[r, TX - 1 - j if mirror else j] * source[r, first + j : first + j + n, at]
            rows = pl.ds(pl.multiple_of(r * 128 + t * 16, 16), 16)
            by_x[first : first + n, rows, :] = total

    def along_yx(kind, y_spans, x_spans):
        mirror = kind == 0
        for span in y_spans:
            y_piece(0, 0, by_a, kind, *span)

        def two(n, carry):
            for span in y_spans:
                y_piece(2 * n + 1, n, by_b, kind, *span)
            for span in x_spans:
                x_piece(2 * n, n, by_a, mirror, *span)
            later = jnp.minimum(n + 1, 3)
            for span in y_spans:
                y_piece(2 * later, later, by_a, kind, *span)
            for span in x_spans:
                x_piece(2 * n + 1, n, by_b, mirror, *span)
            return carry

        lax.fori_loop(0, 4, two, 0)

    def along_z(k, kind):
        results = []
        for j in range(0, 8, 2):
            x = k * 8 + j
            hi = jnp.concatenate([x_hi[x], x_hi[x + 1]], axis=1)
            lo = jnp.concatenate([x_lo[x], x_lo[x + 1]], axis=1)
            both = dot(bz_hl[kind], hi)
            total = both[0:128] + both[128:256] + dot(bz_hl[kind, 0:128], lo)
            results += [total[:, 0:128], total[:, 128:256]]
        return results

    def in_order(j):
        return jnp.where(j == 0, 0, jnp.where(j == 1, 3, j - 1))

    def keep_columns(k, values):
        pairs = [split(v) for v in values]
        for s in range(8):
            e_hi[7 + k * 8 + s] = pairs[s][0]
            e_lo[7 + k * 8 + s] = pairs[s][1]

    onehot = onehot_of(labels)

    def start_group(j, carry):
        k = in_order(j)
        values = []
        for p in range(4):
            both = dot(onehot, received[:, k * 4 + p].reshape(NB * 16, 128))
            values += [both[0:128], both[128:256]]
        for s in range(8):
            observed[k * 8 + s] = values[s].astype(BF)
        emit(0, k, values)
        values = [v + dark_col[...] for v in values]
        for s in range(8):
            estimate[k * 8 + s] = values[s]
        keep_columns(k, values)
        return carry

    lax.fori_loop(0, 4, start_group, 0)
    emit_corners(0)

    for i in range(STEPS):
        kind = i % 2
        last = i == STEPS - 1
        moves = all_moves(i)
        along_yx(kind, [(7, 32)], [(7, 5), (12, 4), (16, 5), (21, 4)])
        for m in moves[0:8]:
            m.wait_recv()

        def main_rim(k, carry, i=i, kind=kind):
            rim_y(i, k + 1, kind, None)
            return carry

        lax.fori_loop(0, 4, main_rim, 0)
        for m in moves[8:10]:
            m.wait_recv()
        for side, members, at, keep in ((0, range(1, 8), 0, b > 0), (1, range(0, 7), 39, b < NB - 1)):
            for n, s in enumerate(members):
                v = x_halo[i, side, s].astype(F32)
                if i == 0:
                    v += dark_col[...]
                v = jnp.where(keep, v, 0.0)
                if i == 0:
                    e_hi[at + n], e_lo[at + n] = split(v)
                else:
                    e_hi[at + n] = v.astype(BF)
                    e_lo[at + n] = jnp.zeros((128, 128), BF)
        along_yx(kind, [(0, 7), (39, 7)], [(0, 4), (4, 3), (25, 4), (29, 3)])
        for m in moves[10:]:
            m.wait_recv()
        rim_y(i, 0, kind, b > 0)
        rim_y(i, 5, kind, b < NB - 1)
        rim_x(kind == 0)
        lax.fori_loop(0, 4, add_rim, 0)

        def end_group(j, carry, i=i, kind=kind, last=last):
            k = in_order(j)
            results = along_z(k, kind)
            values = []
            for s in range(8):
                x = k * 8 + s
                if kind == 0:
                    value = observed[x].astype(F32) / (results[s] + dark_col[...])
                else:
                    value = estimate[x] * results[s]
                    if last:
                        final[pl.ds(x, 128, stride=XB), :] = value
                        top[...] = jnp.maximum(top[...], value)
                    else:
                        estimate[x] = value
                values.append(value)
            if not last:
                emit(i + 1, k, values)
                keep_columns(k, values)
            return carry

        lax.fori_loop(0, 4, end_group, 0)
        if not last:
            emit_corners(i + 1)


    highest = jnp.max(top[...])
    scale = 2.0**15 / jnp.where(highest > 0.0, highest, 1.0)
    peak[...] = jnp.full((1, 128), highest, F32)

    def encode(n, carry):
        part = final[pl.ds(pl.multiple_of(n * 256, 256), 256), :] * scale
        part = part * part
        part = part * part
        coded[pl.ds(n * 8, 8)] = (part * part).astype(BF).reshape(8, XB, 128)
        return carry

    lax.fori_loop(0, NZ // 8, encode, 0)
    rows = pl.ds(pl.multiple_of(b * XB, XB), XB)

    def pair(target):
        big = pltpu.make_async_remote_copy(
            src_ref=coded.at[pl.ds(target * 4, 4)],
            dst_ref=out.at[:, rows, :],
            send_sem=send_big.at[target],
            recv_sem=recv_big.at[g],
            device_id=(target, q),
            device_id_type=MESH,
        )
        small = pltpu.make_async_remote_copy(
            src_ref=peak,
            dst_ref=peaks.at[b],
            send_sem=send_small.at[target],
            recv_sem=recv_small.at[g],
            device_id=(target, q),
            device_id_type=MESH,
        )
        return big, small

    def pair_from(source):
        block = snake(source)
        big = pltpu.make_async_remote_copy(
            src_ref=coded.at[pl.ds(0, 4)],
            dst_ref=out.at[:, pl.ds(pl.multiple_of(block * XB, XB), XB), :],
            send_sem=send_big.at[source],
            recv_sem=recv_big.at[source],
            device_id=(source, q),
            device_id_type=MESH,
        )
        small = pltpu.make_async_remote_copy(
            src_ref=peak,
            dst_ref=peaks.at[block],
            send_sem=send_small.at[source],
            recv_sem=recv_small.at[source],
            device_id=(source, q),
            device_id_type=MESH,
        )
        return big, small

    def start(m, carry):
        for n in (1, 3, 2):
            for copy in pair(lax.rem(g + 8 * n, NB) // 8 * 8 + lax.rem(g + m, 8)):
                copy.start()
        return carry

    lax.fori_loop(0, 8, start, 0)

    def start_own(m, carry):
        for copy in pair(g // 8 * 8 + lax.rem(g + m, 8)):
            copy.start()
        return carry

    lax.fori_loop(1, 8, start_own, 0)
    mine = (
        pltpu.make_async_copy(coded.at[pl.ds(g * 4, 4)], out.at[:, rows, :], own.at[0]),
        pltpu.make_async_copy(peak, peaks.at[b], own.at[1]),
    )
    for copy in mine:
        copy.start()

    def sent(k, carry):
        target = lax.rem(g + k, NB)
        block_to(target).wait_send()
        label_to(target).wait_send()
        return carry

    lax.fori_loop(1, NB, sent, 0)
    for i in range(STEPS):
        for m in all_moves(i):
            m.wait_send()
    for copy in mine:
        copy.wait()

    def finish(k, carry):
        other = lax.rem(g + k, NB)
        for copy in pair(other):
            copy.wait_send()
        for copy in pair_from(other):
            copy.wait_recv()
        return carry

    lax.fori_loop(1, NB, finish, 0)


def decode_kernel(coded, peaks, out):
    for n in range(NB):
        at = pl.ds(n * XB, XB)
        root = lax.rsqrt(lax.rsqrt(jnp.maximum(coded[0, at].astype(F32), 2.0**-120)))
        out[0, at] = root * lax.rsqrt(root) * (peaks[n] * 2.0**-15)


def decode(coded, peaks):
    return pl.pallas_call(
        decode_kernel,
        grid=(coded.shape[0],),
        out_shape=jax.ShapeDtypeStruct(coded.shape, F32),
        in_specs=[
            pl.BlockSpec((1,) + coded.shape[1:], lambda i: (i, 0, 0)),
            pl.BlockSpec(peaks.shape, lambda i: (0, 0, 0)),
        ],
        out_specs=pl.BlockSpec((1,) + coded.shape[1:], lambda i: (i, 0, 0)),
        compiler_params=params(8),
        name="decode",
    )(coded, peaks)


def shards(raw_planes, slot_plane, shear_offsets, dark_level, profile_z, profile_x, profile_y):
    columns = raw_planes.shape[1]
    dma = pltpu.SemaphoreType.DMA
    vmem = pltpu.VMEM
    coded, peaks = pl.pallas_call(
        whole_kernel,
        out_shape=[
            jax.ShapeDtypeStruct((4, columns, 128), BF),
            jax.ShapeDtypeStruct((NB, 1, 128), F32),
        ],
        in_specs=[SM] * 5 + [ANY, V],
        out_specs=[ANY, ANY],
        scratch_shapes=[
            vmem((CAP, columns, 128), BF),
            vmem((CAP, SHEAR + columns, 128), F32),
            vmem((ROWS * CAP, 128), F32),
            vmem((columns // 2, 16, 128), BF),
            vmem((1, 128), I32),
            vmem((NB, 16, 16, 128), BF),
            vmem((NB, 1, 128), I32),
            vmem((2, 384, 256), BF),
            vmem((2, 256, 256), BF),
            vmem((8, 128, 128), BF),
            vmem((2, 256, 256), BF),
            vmem((128, 128), F32),
            vmem((128, 128), F32),
            vmem((XB, 128, 128), BF),
            vmem((XB, 128, 128), F32),
            vmem((WIDE, 128, 128), BF),
            vmem((WIDE, 128, 128), BF),
            vmem((2, WIDE, 64, 128), F32),
            vmem((2, WIDE, 64, 128), F32),
            vmem((XB, 256, 128), F32),
            vmem((2, 48, 16, 128), F32),
            vmem((2, XB, 16, 256), BF),
            vmem((XB, 256, 128), BF),
            vmem((XB, 256, 128), BF),
            vmem((STEPS, 2, 8, 128, 128), BF),
            vmem((STEPS, 4, 128, 128), BF),
            vmem((STEPS, 2, 8, 128, 128), BF),
            vmem((STEPS, 2, 6, 128, 128), BF),
            vmem((NZ, XB, 128), BF),
            vmem((1, 128), F32),
            vmem((NZ * XB, 128), F32),
            vmem((128, 128), F32),
            dma((CAP,)),
            dma((NB,)),
            dma((NB,)),
            dma((NB,)),
            dma((NB,)),
            dma((STEPS, MOVES)),
            dma((STEPS, MOVES)),
            dma((NB,)),
            dma((NB,)),
            dma((NB,)),
            dma((NB,)),
            dma((2,)),
        ],
        compiler_params=params(56, collective_id=0, has_side_effects=True),
        name="deconvolve",
    )(slot_plane, shear_offsets, profile_z, profile_x, profile_y, raw_planes, dark_level.reshape(1, 128))
    return decode(coded, peaks)


def solution(mesh):
    in_specs = (P("gz", None, "gy"), P("gz"), P(), P(), P(), P(), P())
    out_specs = P("gz", None, "gy")
    return jax.shard_map(shards, mesh=mesh, in_specs=in_specs, out_specs=out_specs, check_vma=False)
```

time: 178 us -> 152 us (0.85)
  Pallas kernels: 171 us -> 150 us
  other arithmetic: 2.9 us -> 0 us
    pallas_call x4 -> x2, Pallas kernels: 171 us -> 150 us  [the longest x1 148 us: shards(): pl.pallas_call(whole_kernel, out_shape=[jax.ShapeDtypeStruct((4, columns,...]
    mul x2 -> x0, other arithmetic: 2.9 us -> none  [the longest x1 2.88 us: shards(): jnp.sqrt(jnp.sqrt(jnp.sqrt(coded.astype(F32)))).reshape(4, NB, XB, 128)]
where the time goes in v3:
time: 152 us
  Pallas kernels  150 us (99%)
  local copies, waits for them, and re-layouts  1.93 us (1%)
    pallas_call x1, Pallas kernels, shards(): pl.pallas_call(whole_kernel, out_shape=[jax.ShapeDtypeStruct((4, columns,...  148 us

profile of v3, /device:TPU:23, one launch (start us, length us, event | category | flops | bytes accessed | tf_op | source)
XLA Modules:
  0.0 152.2 jit_solution(5483775838881915044)
XLA Ops:
  0.0 148.0 %deconvolve.1 = (bf16[4,1024,128]{2,1,0:T(8,128)(2,1)}, f32[32,1,128]{2,1,0:T(1,128)}) custom-call(s32[8]{0:T(128)} %slot.1, s32[128]{0:T(128)} %offsets.1, f32[2,41]{1,0:T(2,128)} %pz.1, f32[2,15]{1,0:T(2,128)} %px.1, f32[2,15]{1,0:T(2,128)} %py.1, bf16[8,1024,128]{2,1,0:T(8,128)(2,1)} %raw_hbm.1, f32[1,128]{1,0:T(1,128)} %bitcast.1), custom_call_target="tpu_custom_call" | custom-call | tf_op jit(solution)/shard_map/deconvolve/pallas_call | solution.py:614
  148.0 0.0 copy-start
  148.0 1.2 copy-done
  149.2 0.0 copy-start.1
  149.2 0.7 copy-done.1
  150.0 2.3 %decode.1 = f32[4,1024,128]{2,1,0:T(8,128)} custom-call(bf16[4,1024,128]{2,1,0:T(8,128)(2,1)S(1)} %copy-done, f32[32,1,128]{2,1,0:T(1,128)S(1)} %copy-done.1), custom_call_target="tpu_custom_call" | custom-call | tf_op jit(solution)/shard_map/decode/pallas_call | solution.py:596
Async XLA Ops:
  148.0 1.2 copy-start
  149.2 0.7 copy-start.1

commit v4 on v3

--- a/solution.py
+++ b/solution.py
@@ -285,27 +285,23 @@
 
     chunk_of_lane = lax.div(iota((16, 128), 1), 16)
 
-    def emit(i, k, values):
-        @pl.when(k == 0)
-        def _():
-            for s in range(8):
-                faces[i, 0, s] = values[s].astype(BF)
-            face_down(i).start()
-
-        @pl.when(k == 3)
-        def _():
-            for s in range(8):
-                faces[i, 1, s] = values[s].astype(BF)
-            face_up(i).start()
-
+    def pack(i, k, values):
         for c in range(8):
             tile = jnp.zeros((16, 128), F32)
             for n in range(8):
                 turned = pltpu.roll(values[c][n * 16 : n * 16 + 16], (n * 16 + 8) % 128, 1)
                 tile = jnp.where(chunk_of_lane == n, turned, tile)
             packs[i, k, c * 16 : c * 16 + 16] = tile.astype(BF)
-        for m in pack_moves(i, k):
-            m.start()
+
+    def emit(i, j):
+        @pl.when(j == 0)
+        def _():
+            face_down(i).start()
+            face_up(i).start()
+
+        for k in (j, 3 - j):
+            for m in pack_moves(i, k):
+                m.start()
 
     def emit_corners(i):
         for m in first_corners(i) + last_corners(i):
@@ -315,17 +311,20 @@
     lane16 = lax.rem(lane, 16)
     outside_y = ((lane16 < 8) & (q == 0)) | ((lane16 >= 8) & (q == count - 1))
 
-    def rim_y(i, group, kind, keep):
-        halo = jnp.where(lane16 < 8, y_halo[i, 0, group].astype(F32), y_halo[i, 1, group].astype(F32))
+    def rim_y(i, group, n, kind, keep):
+        outside = jnp.concatenate([outside_y] * n, axis=0)
+        before = jnp.concatenate([lane16 < 8] * n, axis=0)
+        sides = [y_halo[i, side, group : group + n].reshape(n * 128, 128).astype(F32) for side in range(2)]
+        halo = jnp.where(before, sides[0], sides[1])
         if i == 0:
-            halo += dark_pack[...]
-        halo = jnp.where(outside_y, 0.0, halo)
+            halo += jnp.concatenate([dark_pack[...]] * n, axis=0)
+        halo = jnp.where(outside, 0.0, halo)
         if keep is not None:
             halo = jnp.where(keep, halo, 0.0)
         halo = halo.astype(BF)
         total = dot(jnp.concatenate([halo, halo], axis=1), wh[kind])
         for r in range(2):
-            y_rim[r, pl.ds(group * 8, 8)] = total[:, r * 128 : r * 128 + 128].reshape(8, 16, 128)
+            y_rim[r, group * 8 : (group + n) * 8] = total[:, r * 128 : r * 128 + 128].reshape(n * 8, 16, 128)
 
     def rim_x(mirror):
         for r in range(2):
@@ -398,9 +397,6 @@
             results += [total[:, 0:128], total[:, 128:256]]
         return results
 
-    def in_order(j):
-        return jnp.where(j == 0, 0, jnp.where(j == 1, 3, j - 1))
-
     def keep_columns(k, values):
         pairs = [split(v) for v in values]
         for s in range(8):
@@ -409,22 +405,31 @@
 
     onehot = onehot_of(labels)
 
-    def start_group(j, carry):
-        k = in_order(j)
-        values = []
-        for p in range(4):
-            both = dot(onehot, received[:, k * 4 + p].reshape(NB * 16, 128))
-            values += [both[0:128], both[128:256]]
-        for s in range(8):
-            observed[k * 8 + s] = values[s].astype(BF)
-        emit(0, k, values)
-        values = [v + dark_col[...] for v in values]
-        for s in range(8):
-            estimate[k * 8 + s] = values[s]
-        keep_columns(k, values)
-        return carry
-
-    lax.fori_loop(0, 4, start_group, 0)
+    def store_faces(i, j, first, second):
+        @pl.when(j == 0)
+        def _():
+            for s in range(8):
+                faces[i, 0, s] = first[s]
+                faces[i, 1, s] = second[s]
+
+    def start_groups(j, carry):
+        for k in (j, 3 - j):
+            values = []
+            for p in range(4):
+                both = dot(onehot, received[:, k * 4 + p].reshape(NB * 16, 128))
+                values += [both[0:128], both[128:256]]
+            for s in range(8):
+                observed[k * 8 + s] = values[s].astype(BF)
+            pack(0, k, values)
+            values = [v + dark_col[...] for v in values]
+            for s in range(8):
+                estimate[k * 8 + s] = values[s]
+            keep_columns(k, values)
+        store_faces(0, j, [observed[s] for s in range(8)], [observed[XB - 8 + s] for s in range(8)])
+        emit(0, j)
+        return carry
+
+    lax.fori_loop(0, 2, start_groups, 0)
     emit_corners(0)
 
     for i in range(STEPS):
@@ -435,11 +440,7 @@
         for m in moves[0:8]:
             m.wait_recv()
 
-        def main_rim(k, carry, i=i, kind=kind):
-            rim_y(i, k + 1, kind, None)
-            return carry
-
-        lax.fori_loop(0, 4, main_rim, 0)
+        rim_y(i, 1, 4, kind, None)
         for m in moves[8:10]:
             m.wait_recv()
         for side, members, at, keep in ((0, range(1, 8), 0, b > 0), (1, range(0, 7), 39, b < NB - 1)):
@@ -452,37 +453,43 @@
                     e_hi[at + n], e_lo[at + n] = split(v)
                 else:
                     e_hi[at + n] = v.astype(BF)
-                    e_lo[at + n] = jnp.zeros((128, 128), BF)
+                    if i == 1:
+                        e_lo[at + n] = jnp.zeros((128, 128), BF)
         along_yx(kind, [(0, 7), (39, 7)], [(0, 4), (4, 3), (25, 4), (29, 3)])
         for m in moves[10:]:
             m.wait_recv()
-        rim_y(i, 0, kind, b > 0)
-        rim_y(i, 5, kind, b < NB - 1)
+        rim_y(i, 0, 1, kind, b > 0)
+        rim_y(i, 5, 1, kind, b < NB - 1)
         rim_x(kind == 0)
         lax.fori_loop(0, 4, add_rim, 0)
 
-        def end_group(j, carry, i=i, kind=kind, last=last):
-            k = in_order(j)
-            results = along_z(k, kind)
-            values = []
-            for s in range(8):
-                x = k * 8 + s
-                if kind == 0:
-                    value = observed[x].astype(F32) / (results[s] + dark_col[...])
-                else:
-                    value = estimate[x] * results[s]
-                    if last:
-                        final[pl.ds(x, 128, stride=XB), :] = value
-                        top[...] = jnp.maximum(top[...], value)
+        def end_groups(j, carry, i=i, kind=kind, last=last):
+            for k in (j, 3 - j):
+                results = along_z(k, kind)
+                values = []
+                for s in range(8):
+                    x = k * 8 + s
+                    if kind == 0:
+                        value = observed[x].astype(F32) / (results[s] + dark_col[...])
                     else:
-                        estimate[x] = value
-                values.append(value)
+                        value = estimate[x] * results[s]
+                        if last:
+                            final[pl.ds(x, 128, stride=XB), :] = value
+                            top[...] = jnp.maximum(top[...], value)
+                        else:
+                            estimate[x] = value
+                    values.append(value)
+                if not last:
+                    pack(i + 1, k, values)
+                    keep_columns(k, values)
             if not last:
-                emit(i + 1, k, values)
-                keep_columns(k, values)
+                store_faces(
+                    i + 1, j, [e_hi[7 + s] for s in range(8)], [e_hi[7 + XB - 8 + s] for s in range(8)]
+                )
+                emit(i + 1, j)
             return carry
 
-        lax.fori_loop(0, 4, end_group, 0)
+        lax.fori_loop(0, 2, end_groups, 0)
         if not last:
             emit_corners(i + 1)
 
@@ -588,21 +595,21 @@
 def decode_kernel(coded, peaks, out):
     for n in range(NB):
         at = pl.ds(n * XB, XB)
-        root = lax.rsqrt(lax.rsqrt(jnp.maximum(coded[0, at].astype(F32), 2.0**-120)))
-        out[0, at] = root * lax.rsqrt(root) * (peaks[n] * 2.0**-15)
+        root = lax.rsqrt(lax.rsqrt(jnp.maximum(coded[:, at].astype(F32), 2.0**-120)))
+        out[:, at] = root * lax.rsqrt(root) * (peaks[n] * 2.0**-15)
 
 
 def decode(coded, peaks):
     return pl.pallas_call(
         decode_kernel,
-        grid=(coded.shape[0],),
+        grid=(coded.shape[0] // 2,),
         out_shape=jax.ShapeDtypeStruct(coded.shape, F32),
         in_specs=[
-            pl.BlockSpec((1,) + coded.shape[1:], lambda i: (i, 0, 0)),
+            pl.BlockSpec((2,) + coded.shape[1:], lambda i: (i, 0, 0)),
             pl.BlockSpec(peaks.shape, lambda i: (0, 0, 0)),
         ],
-        out_specs=pl.BlockSpec((1,) + coded.shape[1:], lambda i: (i, 0, 0)),
-        compiler_params=params(8),
+        out_specs=pl.BlockSpec((2,) + coded.shape[1:], lambda i: (i, 0, 0)),
+        compiler_params=params(60),
         name="decode",
     )(coded, peaks)
 

time: 152 us -> 151 us (level)
  local copies, waits for them, and re-layouts: 1.93 us -> 0 us
    unnamed x4 -> x0, local copies, waits for them, and re-layouts: 1.93 us -> none
where the time goes in v4:
time: 151 us; the launch traced here: 150 us
  Pallas kernels  150 us (99%)
    pallas_call x1, Pallas kernels, shards(): pl.pallas_call(whole_kernel, out_shape=[jax.ShapeDtypeStruct((4, columns,...  147 us

profile of v4, /device:TPU:23, one launch (start us, length us, event | category | flops | bytes accessed | tf_op | source)
XLA Modules:
  0.0 149.7 jit_solution(4424947142545472180)
XLA Ops:
  0.0 146.8 %deconvolve.1 = (bf16[4,1024,128]{2,1,0:T(8,128)(2,1)}, f32[32,1,128]{2,1,0:T(1,128)}) custom-call(s32[8]{0:T(128)} %slot.1, s32[128]{0:T(128)} %offsets.1, f32[2,41]{1,0:T(2,128)} %pz.1, f32[2,15]{1,0:T(2,128)} %px.1, f32[2,15]{1,0:T(2,128)} %py.1, bf16[8,1024,128]{2,1,0:T(8,128)(2,1)} %raw_hbm.1, f32[1,128]{1,0:T(1,128)} %bitcast.1), custom_call_target="tpu_custom_call" | custom-call | tf_op jit(solution)/shard_map/deconvolve/pallas_call | solution.py:621
  146.9 2.9 %decode.1 = f32[4,1024,128]{2,1,0:T(8,128)} custom-call(bf16[4,1024,128]{2,1,0:T(8,128)(2,1)} %get-tuple-element.7.coded, f32[32,1,128]{2,1,0:T(1,128)} %get-tuple-element.8.peaks), custom_call_target="tpu_custom_call" | custom-call | tf_op jit(solution)/shard_map/decode/pallas_call | solution.py:603
